TPU v7x, 128 devices: a whole 4x4x4 slice. The times are simulated.
128 devices in a mesh: grp: 2 (over y_lo), row: 8 (over x, core), col: 8 (over z, y_hi).
Axes of the slice: x: 4, y: 4 (y_hi: 2, y_lo: 2; y = y_hi * 2 + y_lo), z: 4, core: 2. Of those that a mesh axis runs over, the one named last changes fastest.
Arguments:
- root_inverse: float32 [4096, 4096], P('row', ('grp', 'col')), as said below
- ancestor_map: int32 [2, 2048], P('grp'), may hold values from 0 to 4095, as said below
- live_rows: int32 [2], P('grp'), may hold values from 512 to 2048, as said below
- factor_below: float32 [2, 2048, 3072], P('grp', 'row', 'col'), may hold values from -0.125 to 0.125
- diag_inverse: float32 [2, 3072, 3072], P('grp', 'row', 'col'), as said below
- tile_mask: int32 [2, 16, 24], P('grp', 'row', 'col'), may hold values 0 or 1
Outputs:
- below_inverse: float32 [2, 2048, 3072], P('grp', 'row', 'col')
- separator_inverse: float32 [2, 3072, 3072], P('grp', 'row', 'col')
Inputs may be any that keep to these rules, and one draw needn't show every extreme that they name: `ancestor_map`: within each front the map's 2048 entries are distinct root rows in an order drawn from the seed; 0 and 4095 are among them. `live_rows`: front 0 uses all 2048 rows. `root_inverse`: symmetric with a positive diagonal. `diag_inverse`: lower triangular with a positive diagonal.
All inputs are finite; a program needn't handle non-finite values. No bound on the sum of `tile_mask` on one device may be relied on, other than what follows from the above.
Results may differ from a plain program's by a relative error of at most 0.0001.
Values sent between devices are 32-bit elements; how exact they have to be, the bound alone decides.
No kernel may reach another device: no remote copies, remote signals or barrier semaphores. Data moves between devices by JAX's collectives and lax.ppermute only.
A program may use at most 128 MiB of HBM per device.

v0:
```python
import jax
import jax.numpy as jnp
from jax import lax
from jax.sharding import PartitionSpec as P

ROOT = 4096
SEP = 3072
ANC = 2048
TILE = 128


highest = lax.Precision.HIGHEST
inner_dims = (((0,), (0,)), ((), ()))


def per_device(root_inverse, ancestor_map, live_rows, factor_below, diag_inverse, tile_mask):
    tile_keep = jnp.repeat(jnp.repeat(tile_mask[0], TILE, axis=0), TILE, axis=1).astype(jnp.float32)
    retained = factor_below[0] * tile_keep
    diag_block = diag_inverse[0]
    band_rows = retained.shape[0]
    col_width = diag_block.shape[1]
    retained_full, diag_full = (
        lax.all_gather(retained, "col", axis=1, tiled=True),
        lax.all_gather(diag_block, "col", axis=1, tiled=True),
    )
    update = jnp.dot(
        retained_full,
        lax.all_gather(diag_block, "row", axis=0, tiled=True),
        precision=highest,
        preferred_element_type=jnp.float32,
    )
    live_count = live_rows[0]
    first_row = lax.axis_index("row") * band_rows
    band_ids = first_row + jnp.arange(band_rows, dtype=jnp.int32)
    update = jnp.where(band_ids[:, None] < live_count, update, jnp.float32(0.0))
    panel = lax.all_gather(update, "row", axis=0, tiled=True)
    ancestor_ids = ancestor_map[0]
    spread = jnp.zeros((ROOT, col_width), jnp.float32).at[ancestor_ids].add(panel)
    product = jnp.dot(
        lax.all_gather(root_inverse, ("grp", "col"), axis=1, tiled=True),
        spread,
        precision=highest,
        preferred_element_type=jnp.float32,
    )
    product_all = lax.all_gather(product, "row", axis=0, tiled=True)
    live_flag = jnp.arange(ANC, dtype=jnp.int32) < live_count
    coupling_all = jnp.where(live_flag[:, None], -product_all[ancestor_ids], jnp.float32(0.0))
    coupling = lax.dynamic_slice_in_dim(coupling_all, first_row, band_rows, 0)
    update_full = lax.all_gather(update, "col", axis=1, tiled=True)
    share_rows = SEP // lax.axis_size("row")
    gram = lax.dot_general(
        diag_full, diag_block, inner_dims, precision=highest, preferred_element_type=jnp.float32
    )
    cross = lax.dot_general(
        update_full, coupling, inner_dims, precision=highest, preferred_element_type=jnp.float32
    )
    summed = lax.psum(gram - cross, "row")
    separator = lax.dynamic_slice_in_dim(summed, lax.axis_index("row") * share_rows, share_rows, 0)
    return (coupling[None], separator[None])


def solution(mesh):
    return jax.shard_map(
        per_device,
        mesh=mesh,
        in_specs=(
            P("row", ("grp", "col")),
            P("grp", None),
            P("grp"),
            P("grp", "row", "col"),
            P("grp", "row", "col"),
            P("grp", "row", "col"),
        ),
        out_specs=(P("grp", "row", "col"), P("grp", "row", "col")),
        check_vma=False,
    )
```

profile of v0, /device:TPU:0, one launch (start us, length us, event | category | flops | bytes accessed | tf_op | source)
XLA Modules:
  0.0 650.0 jit_solution(16598959246190883008)
XLA Ops:
  7.2 1.2 copy.9
  8.4 0.7 convert_bitcast_fusion
  9.1 0.1 copy.10
  9.2 0.1 broadcast_bitcast_fusion
  9.2 0.8 bitcast_multiply_fusion
  10.0 0.0 all-gather.20.cloned.1.call-start
  10.1 0.7 all-gather.20.cloned.1.call-update
  11.5 64.7 %all-gather.10.cloned.1.call-done = f32[256,3072]{0,1:T(8,128)} async-done(((f32[256,384]{0,1:T(8,128)}), f32[256,3072]{0,1:T(8,128)}) %all-gather.10.cloned.1.call-update) | async-done | bytes 3145744 | tf_op jit(solution)/shard_map/all_gather | solution.py:23
  76.2 33.7 %all-gather.20.cloned.1.call-done = f32[1,3072,384]{2,1,0:T(8,128)} async-done(((f32[1,384,384]{2,1,0:T(8,128)}), f32[1,3072,384]{2,1,0:T(8,128)}) %all-gather.20.cloned.1.call-update) | async-done | bytes 4718608 | tf_op jit(solution)/shard_map/all_gather | solution.py:28
  109.9 9.2 %fusion.9 = f32[256,384]{1,0:T(8,128)} fusion(f32[256,3072]{0,1:T(8,128)} %all-gather.10.cloned.1.call-done, f32[1,3072,384]{2,1,0:T(8,128)} %all-gather.20.cloned.1.call-done, pred[256]{0:T(512)(128)(4,1)S(1)} %add_compare_fusion), kind=kOutput, calls=%fused_computation.10 | convolution fusion | flops 3623976960 | bytes 8257792 | tf_op jit(solution)/shard_map/dot_general | solution.py:26
  119.2 0.0 all-gather.14.cloned.1.call-start
  119.2 0.5 all-gather.14.cloned.1.call-update
  119.7 0.0 all-gather.16.cloned.1.call-start
  119.8 27.2 %all-gather.12.cloned.1.call-done = f32[2048,384]{1,0:T(8,128)} async-done(((f32[256,384]{1,0:T(8,128)}), f32[2048,384]{1,0:T(8,128)}) %all-gather.12.cloned.1.call-update) | async-done | bytes 3145744 | tf_op jit(solution)/shard_map/all_gather | solution.py:36
  147.0 16.2 %scatter_custom_fusion = f32[4096,384]{1,0:T(8,128)} fusion(s32[2048]{0:T(1024)S(1)} %bitcast.42, f32[2048,384]{1,0:T(8,128)} %all-gather.12.cloned.1.call-done, f32[]{:T(128)} %constant.9.clone.1), kind=kCustom, calls=%fused_computation.7 | custom fusion | flops 786432 | bytes 6291968 | tf_op jit(solution)/shard_map/scatter-add | solution.py:38
  163.2 183.9 %all-gather.14.cloned.1.call-done = f32[512,4096]{1,0:T(8,128)} async-done(((f32[512,256]{1,0:T(8,128)}), f32[512,4096]{1,0:T(8,128)}) %all-gather.14.cloned.1.call-update) | async-done | bytes 8388624 | tf_op jit(solution)/shard_map/all_gather | solution.py:40
  347.1 24.0 %convolution_bitcast_fusion = f32[512,384]{0,1:T(8,128)} fusion(f32[4096,384]{1,0:T(8,128)} %scatter_custom_fusion, f32[512,4096]{1,0:T(8,128)} %all-gather.14.cloned.1.call-done), kind=kOutput, calls=%fused_computation.9 | convolution fusion | flops 9663676416 | bytes 15466496 | tf_op jit(solution)/shard_map/dot_general | solution.py:39
  371.2 0.0 all-gather.18.cloned.1.call-start
  371.2 0.5 all-gather.18.cloned.1.call-update
  371.8 0.7 all-gather.22.cloned.1.call-update
  372.5 0.3 all-reduce.2.cloned.1.call-start
  372.8 0.1 dynamic-slice
  372.8 42.6 %all-gather.16.cloned.1.call-done = f32[4096,384]{0,1:T(8,128)} async-done(((f32[512,384]{0,1:T(8,128)}), f32[4096,384]{0,1:T(8,128)}) %all-gather.16.cloned.1.call-update) | async-done | bytes 6291472 | tf_op jit(solution)/shard_map/all_gather | solution.py:45
  415.4 6.5 %copy.11 = f32[4096,384]{1,0:T(8,128)} copy(f32[4096,384]{0,1:T(8,128)} %all-gather.16.cloned.1.call-done) | data formatting | bytes 12582912 | tf_op jit(solution)/shard_map/all_gather | solution.py:45
  422.0 11.9 %gather_fusion = f32[2048,384]{1,0:T(8,128)} fusion(f32[4096,384]{1,0:T(8,128)} %copy.11, s32[2048]{0:T(1024)S(1)} %broadcast_clamp_fusion), kind=kCustom, calls=%fused_computation | custom fusion | bytes 6299648 | tf_op jit(solution)/shard_map/gather | solution.py:47
  433.9 46.9 %all-gather.18.cloned.1.call-done = f32[256,3072]{1,0:T(8,128)} async-done(((f32[256,384]{1,0:T(8,128)}), f32[256,3072]{1,0:T(8,128)}) %all-gather.18.cloned.1.call-update) | async-done | bytes 3145744 | tf_op jit(solution)/shard_map/all_gather | solution.py:49
  480.8 8.4 %fusion.15 = f32[3072,384]{1,0:T(8,128)} fusion(f32[256,3072]{1,0:T(8,128)} %all-gather.18.cloned.1.call-done, f32[2048,384]{1,0:T(8,128)} %gather_fusion, s32[]{:T(128)S(6)} %select_n.28, pred[256]{0:T(512)(128)(4,1)S(1)} %dynamic-slice), kind=kOutput, calls=%fused_computation.17 | convolution fusion | flops 3624075264 | bytes 8257796 | tf_op jit(solution)/shard_map/dot_general | solution.py:54
  489.3 67.2 %all-gather.22.cloned.1.call-done = f32[1,384,3072]{2,1,0:T(8,128)} async-done(((f32[1,384,384]{2,1,0:T(8,128)}), f32[1,384,3072]{2,1,0:T(8,128)}) %all-gather.22.cloned.1.call-update) | async-done | bytes 4718608 | tf_op jit(solution)/shard_map/all_gather | solution.py:24
  556.5 12.4 %fusion.4 = f32[3072,384]{1,0:T(8,128)} fusion(f32[3072,384]{1,0:T(8,128)} %fusion.15, f32[1,384,3072]{2,1,0:T(8,128)} %all-gather.22.cloned.1.call-done, f32[1,384,384]{2,1,0:T(8,128)S(1)} %copy-done), kind=kOutput, calls=%fused_computation.6 | convolution fusion | flops 5436997632 | bytes 14745600 | tf_op jit(solution)/shard_map/dot_general | solution.py:51
  568.9 1.9 fusion.14
  570.7 70.5 %all-reduce.2.cloned.1.call-done = f32[3072,384]{1,0:T(8,128)} async-done(((f32[3072,384]{1,0:T(8,128)}), f32[3072,384]{1,0:T(8,128)}) %all-reduce.2.cloned.1.call-update) | async-done | bytes 4718608 | tf_op jit(solution)/shard_map/psum | solution.py:57
  641.3 1.9 dynamic-slice_bitcast_fusion
  (16 shorter events, 0.2 us)
Async XLA Ops:
  7.2 69.1 %all-gather.10.cloned.1.call-start = ((), (), s32[]{:S(2)}) async-start(), calls=%async_computation | async-start | bytes 3538944 | tf_op jit(solution)/shard_map/all_gather | solution.py:23
  10.0 99.9 %all-gather.20.cloned.1.call-start = ((), (), s32[]{:S(2)}) async-start(), calls=%async_computation.6 | async-start | bytes 5308416 | tf_op jit(solution)/shard_map/all_gather | solution.py:28
  10.8 109.0 %copy-start.1 = (s32[1,2048]{1,0:T(1,128)S(1)}, s32[1,2048]{1,0:T(1,128)}, u32[]{:S(2)}) copy-start(s32[1,2048]{1,0:T(1,128)} %param.7) | copy-start | bytes 24580
  10.8 136.2 %all-gather.12.cloned.1.call-start = ((), (), s32[]{:S(2)}) async-start(), calls=%async_computation.1 | async-start | bytes 3538944 | tf_op jit(solution)/shard_map/all_gather | solution.py:36
  119.2 227.9 %all-gather.14.cloned.1.call-start = ((), (), s32[]{:S(2)}) async-start(), calls=%async_computation.2 | async-start | bytes 8912896 | tf_op jit(solution)/shard_map/all_gather | solution.py:40
  119.7 295.7 %all-gather.16.cloned.1.call-start = ((), (), s32[]{:S(2)}) async-start(), calls=%async_computation.3 | async-start | bytes 7077888 | tf_op jit(solution)/shard_map/all_gather | solution.py:45
  371.2 109.7 %all-gather.18.cloned.1.call-start = ((), (), s32[]{:S(2)}) async-start(), calls=%async_computation.4 | async-start | bytes 3538944 | tf_op jit(solution)/shard_map/all_gather | solution.py:49
  371.7 184.8 %all-gather.22.cloned.1.call-start = ((), (), s32[]{:S(2)}) async-start(), calls=%async_computation.7 | async-start | bytes 5308416 | tf_op jit(solution)/shard_map/all_gather | solution.py:24
  372.5 268.8 %all-reduce.2.cloned.1.call-start = ((), (), s32[]{:S(2)}) async-start(), calls=%async_computation.5 | async-start | bytes 9437184 | tf_op jit(solution)/shard_map/psum | solution.py:57
  433.9 122.6 %copy-start = (f32[1,384,384]{2,1,0:T(8,128)S(1)}, f32[1,384,384]{2,1,0:T(8,128)}, u32[]{:S(2)}) copy-start(f32[1,384,384]{2,1,0:T(8,128)} %param.10) | copy-start | bytes 1769476
Sparse Core Ops, SparseCore 0:
  10.9 65.3 all-gather.9
  77.9 31.9 all-gather.19
  119.3 27.7 all-gather.11
  148.5 198.5 all-gather.13
  371.3 44.1 all-gather.15
  418.2 62.5 all-gather.17
  483.2 73.2 all-gather.21
  569.0 72.2 all-reduce.1
where the time goes:
time: 650 us
  waiting for transfers between devices  539 us (83%)
  matrix products  54 us (8%)
  local copies, waits for them, and re-layouts  21.8 us (3%)
  other arithmetic  19.5 us (3%)
  between operations  14.8 us (2%)
    all_gather x1, waiting for transfers between devices, per_device(): lax.all_gather(root_inverse, ('grp', 'col'), axis=1, tiled=True)  184 us
    psum x1, waiting for transfers between devices, per_device(): summed = lax.psum(gram - cross, 'row')  70.5 us
    all_gather x1, waiting for transfers between devices, per_device(): lax.all_gather(diag_block, 'col', axis=1, tiled=True)  67.2 us
    all_gather x1, waiting for transfers between devices, per_device(): lax.all_gather(retained, 'col', axis=1, tiled=True)  64.7 us
    all_gather x1, waiting for transfers between devices, per_device(): update_full = lax.all_gather(update, 'col', axis=1, tiled=True)  46.9 us
    all_gather x1, waiting for transfers between devices, per_device(): product_all = lax.all_gather(product, 'row', axis=0, tiled=True)  42.6 us
    all_gather x1, waiting for transfers between devices, per_device(): lax.all_gather(diag_block, 'row', axis=0, tiled=True)  33.7 us
    all_gather x1, waiting for transfers between devices, per_device(): panel = lax.all_gather(update, 'row', axis=0, tiled=True)  27.2 us
  transfers between devices with their start and end apart: 8, of which 8 were waited for; matrix products, arithmetic and copies ran while one was open for 7% of the time, Pallas kernels for 0%

commit v1 on v0

v1 whole, which is shorter than its diff:
```python
import functools

import jax
import jax.numpy as jnp
from jax import lax
from jax.experimental import pallas as pl
from jax.experimental.pallas import tpu as pltpu
from jax.sharding import PartitionSpec as P

ROOT = 4096
SEP = 3072
ANC = 2048
TILE = 128
ROWS = 8
COLS = 8
BAND = ANC // ROWS
WIDE = SEP // COLS
KEEP = ROOT // (2 * COLS)

f32 = jnp.float32
bf16 = jnp.bfloat16
VMEM = pl.BlockSpec(memory_space=pltpu.VMEM)
SMEM = pl.BlockSpec(memory_space=pltpu.SMEM)


def shift_z(x, step):
    pairs = [(c, (c // 2 + step) % 4 * 2 + c % 2) for c in range(COLS)]
    return lax.ppermute(x, "col", pairs)


def swap_y(x):
    return lax.ppermute(x, "col", [(c, c ^ 1) for c in range(COLS)])


def swap_group(x):
    return lax.ppermute(x, "grp", [(0, 1), (1, 0)])


COL_ORDER = ((0, 0), (-1, 0), (1, 0), (2, 0), (0, 1), (-1, 1), (1, 1), (2, 1))


def gather_col(x):
    n = x.shape[0] // 2
    before = shift_z(x, 1)
    after = shift_z(x, -1)
    other = swap_y(x)
    far_top = shift_z(before[:n], 1)
    far_low = shift_z(after[n:], -1)
    other_before_low = swap_y(before[n:])
    other_after_top = swap_y(after[:n])
    other_before_top = shift_z(other[:n], 1)
    other_after_low = shift_z(other[n:], -1)
    other_far_top = shift_z(other_before_top, 1)
    other_far_low = shift_z(other_after_low, -1)
    return [
        x[:n], x[n:],
        before[:n], before[n:],
        after[:n], after[n:],
        far_top, far_low,
        other[:n], other[n:],
        other_before_top, other_before_low,
        other_after_top, other_after_low,
        other_far_top, other_far_low,
    ]


def col_ids():
    c = lax.axis_index("col")
    z, y = c // 2, c % 2
    return jnp.stack([(z + dz) % 4 * 2 + jnp.bitwise_xor(y, dy) for dz, dy in COL_ORDER]).astype(jnp.int32)


def split(x):
    high = x.astype(bf16)
    return high, (x - high.astype(f32)).astype(bf16)


def dot(a, b):
    return jnp.dot(a, b, preferred_element_type=f32)


def dot3(a, b):
    return dot(a[0], b[0]) + (dot(a[0], b[1]) + dot(a[1], b[0]))


def params(mib):
    return pltpu.CompilerParams(vmem_limit_bytes=mib * 2**20)


def update_kernel(ids, live, diag, *rest):
    halves, (update_ref, flipped_ref) = rest[:16], rest[16:]
    total = jnp.zeros((BAND, WIDE), f32)
    for p in range(8):
        block = split(diag[pl.ds(pl.multiple_of(ids[p] * WIDE, WIDE), WIDE), :])
        piece = split(jnp.concatenate([halves[2 * p][...], halves[2 * p + 1][...]], axis=0))
        total += dot3(piece, block)
    row = ids[8] + lax.broadcasted_iota(jnp.int32, (BAND, WIDE), 0)
    total = jnp.where(row < live[0], total, 0.0)
    update_ref[...] = total
    flipped_ref[...] = total.T


def pick_kernel(place, *rest):
    halves, (high_ref, low_ref) = rest[:16], rest[16:18]
    source_high, source_low = rest[18:]
    for p in range(16):
        high, low = split(halves[p][...])
        at = p * KEEP
        source_high[:, at:at + KEEP] = high
        source_low[:, at:at + KEEP] = low

    step = 256

    def body(j, carry):
        at = pl.ds(pl.multiple_of(j * step, step), step)
        where = place[:, at]
        hot = jnp.where(lax.broadcasted_iota(jnp.int32, (ROOT, step), 0) == where, 1.0, 0.0).astype(bf16)
        high_ref[:, at] = dot(source_high[...], hot).astype(bf16)
        low_ref[:, at] = dot(source_low[...], hot).astype(bf16)
        return carry

    lax.fori_loop(0, ANC // step, body, 0)


def coupling_kernel(ids, live, high, low, update, out_ref):
    total = jnp.zeros((BAND, WIDE), f32)
    for p in range(4):
        at = slice(p * 512, p * 512 + 512)
        total += dot3((high[:, at], low[:, at]), split(update[at, :]))
    row = ids[8] + lax.broadcasted_iota(jnp.int32, (BAND, WIDE), 0)
    out_ref[...] = jnp.where(row < live[0], -total, 0.0)


def separator_kernel(ids, diag, coupling, *rest):
    diag_halves, update_halves, out_ref = rest[:16], rest[16:32], rest[32]
    n = WIDE // 2
    right_diag, right_coupling = split(diag[...]), split(-coupling[...])
    for p in range(8):
        left = split(jnp.concatenate([diag_halves[2 * p][...], diag_halves[2 * p + 1][...]], axis=0))
        total = dot3(left, right_diag)
        left = split(jnp.concatenate([update_halves[2 * p][...], update_halves[2 * p + 1][...]], axis=0))
        total += dot3(left, right_coupling)
        out_ref[pl.ds(pl.multiple_of(ids[p] * WIDE, WIDE), WIDE), :] = total


def per_device(root_inverse, ancestor_map, live_rows, factor_below, diag_inverse, tile_mask):
    row = lax.axis_index("row")
    group = lax.axis_index("grp")
    first_row = row * BAND
    ids = jnp.concatenate([col_ids(), first_row[None].astype(jnp.int32)])
    diag_block = diag_inverse[0]

    root_cols = lax.all_gather(root_inverse, "row", axis=0, tiled=True)
    diag_cols = lax.all_gather(diag_block, "row", axis=0, tiled=True)

    tile_keep = jnp.repeat(jnp.repeat(tile_mask[0], TILE, axis=0), TILE, axis=1).astype(f32)
    retained = factor_below[0] * tile_keep
    retained_all = gather_col(retained)

    update, update_flipped = pl.pallas_call(
        update_kernel,
        out_shape=(jax.ShapeDtypeStruct((BAND, WIDE), f32), jax.ShapeDtypeStruct((WIDE, BAND), f32)),
        in_specs=[SMEM, SMEM] + [VMEM] * 17,
        out_specs=(VMEM, VMEM),
        compiler_params=params(40),
    )(ids, live_rows, diag_cols, *retained_all)

    own_map = ancestor_map[0]
    other_map = swap_group(own_map)
    own_rows = root_cols[lax.dynamic_slice_in_dim(own_map, first_row, BAND)]
    other_rows = swap_group(root_cols[lax.dynamic_slice_in_dim(other_map, first_row, BAND)])
    picked = gather_col(jnp.concatenate([own_rows, other_rows], axis=0))
    rel = jnp.zeros((COLS,), jnp.int32).at[col_ids()].set(jnp.arange(COLS, dtype=jnp.int32))
    half = (own_map // (ROOT // 2) != group).astype(jnp.int32)
    place = rel[own_map % (ROOT // 2) // KEEP] * (2 * KEEP) + half * KEEP + own_map % KEEP
    high, low = pl.pallas_call(
        pick_kernel,
        out_shape=(jax.ShapeDtypeStruct((BAND, ANC), bf16), jax.ShapeDtypeStruct((BAND, ANC), bf16)),
        in_specs=[VMEM] * 17,
        out_specs=(VMEM, VMEM),
        scratch_shapes=[pltpu.VMEM((BAND, ROOT), bf16), pltpu.VMEM((BAND, ROOT), bf16)],
        compiler_params=params(40),
    )(place[None, :], *picked)

    update_cols = lax.all_gather(update, "row", axis=0, tiled=True)
    coupling = pl.pallas_call(
        coupling_kernel,
        out_shape=jax.ShapeDtypeStruct((BAND, WIDE), f32),
        in_specs=[SMEM, SMEM] + [VMEM] * 3,
        out_specs=VMEM,
        compiler_params=params(40),
    )(ids, live_rows, high, low, update_cols)

    update_all = gather_col(update_flipped)
    diag_all = gather_col(diag_block.T)
    partial = pl.pallas_call(
        separator_kernel,
        out_shape=jax.ShapeDtypeStruct((SEP, WIDE), f32),
        in_specs=[SMEM] + [VMEM] * 34,
        out_specs=VMEM,
        compiler_params=params(48),
    )(ids, diag_block, coupling, *diag_all, *update_all)
    separator = lax.psum_scatter(partial, "row", scatter_dimension=0, tiled=True)
    return (coupling[None], separator[None])


def solution(mesh):
    return jax.shard_map(
        per_device,
        mesh=mesh,
        in_specs=(
            P("row", ("grp", "col")),
            P("grp", None),
            P("grp"),
            P("grp", "row", "col"),
            P("grp", "row", "col"),
            P("grp", "row", "col"),
        ),
        out_specs=(P("grp", "row", "col"), P("grp", "row", "col")),
        check_vma=False,
    )
```

time: 650 us -> 251 us (0.39)
  waiting for transfers between devices: 539 us -> 101 us
  starting transfers between devices: 0.54 us -> 72 us
  matrix products: 54 us -> 0 us
  Pallas kernels: 0 us -> 29.9 us
  other arithmetic: 19.5 us -> 7.05 us
    all_gather x7 -> x3, waiting for transfers between devices: 466 us -> 0.88 us  [the longest x1 0.49 us: per_device(): diag_cols = lax.all_gather(diag_block, 'row', axis=0, tiled=True)]
    ppermute x0 -> x46, starting transfers between devices: none -> 71.9 us  [the longest x32 43.6 us: shift_z(): return lax.ppermute(x, 'col', pairs)]
    psum x1 -> x0, waiting for transfers between devices: 70.5 us -> none  [per_device(): summed = lax.psum(gram - cross, 'row')]
    ppermute x0 -> x46, waiting for transfers between devices: none -> 59 us  [the longest x32 40 us: shift_z(): return lax.ppermute(x, 'col', pairs)]
    dot_general x4 -> x0, matrix products: 54 us -> none  [the longest x1 24 us: per_device(): jnp.dot(lax.all_gather(root_inverse, ('grp', 'col'), axis=1, tiled=True),...]
    reduce_scatter x0 -> x1, waiting for transfers between devices: none -> 39.3 us  [per_device(): lax.psum_scatter(partial, 'row', scatter_dimension=0, tiled=True)]
    pallas_call x0 -> x4, Pallas kernels: none -> 29.9 us  [the longest x1 11.4 us: per_device(): pl.pallas_call(separator_kernel, out_shape=jax.ShapeDtypeStruct((SEP, WID...]
    scatter-add x1 -> x0, other arithmetic: 16.2 us -> none  [per_device(): jnp.zeros((ROOT, col_width), jnp.float32).at[ancestor_ids].add(panel)]
  transfers between devices with their start and end apart: 8 -> 50, of which waited for: 8 -> 24; matrix products, arithmetic and copies ran while one was open for 7% -> 9% of each run, Pallas kernels for 0% -> 7%
where the time goes in v1:
time: 251 us; the launch traced here: 250 us
  waiting for transfers between devices  101 us (40%)
  starting transfers between devices  72 us (29%)
  Pallas kernels  29.9 us (12%)
  local copies, waits for them, and re-layouts  25.6 us (10%)
  between operations  14.8 us (6%)
  other arithmetic  7.05 us (3%)
    ppermute x32, starting transfers between devices, shift_z(): return lax.ppermute(x, 'col', pairs)  43.6 us
    ppermute x32, waiting for transfers between devices, shift_z(): return lax.ppermute(x, 'col', pairs)  40 us
    reduce_scatter x1, waiting for transfers between devices, per_device(): lax.psum_scatter(partial, 'row', scatter_dimension=0, tiled=True)  39.3 us
    ppermute x12, starting transfers between devices, swap_y(): return lax.ppermute(x, 'col', [(c, c ^ 1) for c in range(COLS)])  26.2 us
    unnamed x48, local copies, waits for them, and re-layouts  12.7 us
    pallas_call x1, Pallas kernels, per_device(): pl.pallas_call(separator_kernel, out_shape=jax.ShapeDtypeStruct((SEP, WID...  11.4 us
    pallas_call x1, Pallas kernels, per_device(): pl.pallas_call(pick_kernel, out_shape=(jax.ShapeDtypeStruct((BAND, ANC),...  10.8 us
    ppermute x12, waiting for transfers between devices, swap_y(): return lax.ppermute(x, 'col', [(c, c ^ 1) for c in range(COLS)])  10.5 us
  transfers between devices with their start and end apart: 50, of which 24 were waited for; matrix products, arithmetic and copies ran while one was open for 9% of the time, Pallas kernels for 7%

profile of v1, /device:TPU:0, one launch (start us, length us, event | category | flops | bytes accessed | tf_op | source)
XLA Modules:
  0.0 250.0 jit_solution(9767824326976302297)
XLA Ops:
  10.8 4.2 %collective-permute-start.14 = (f32[256,384]{1,0:T(8,128)S(1)}, f32[256,384]{1,0:T(8,128)S(1)}, u32[]{:S(2)}, u32[]{:S(2)}) collective-permute-start(f32[256,384]{1,0:T(8,128)S(1)} %bitcast_multiply_fusion), channel_id=1, source_target_pairs={{0,6},{1,7},{2,0},{3,1},{4,2},{5,3},{6,4},{7,5},{8,14},{9,15},{10,... | collective-permute-start | bytes 1179656 | tf_op jit(solution)/shard_map/ppermute | solution.py:28
  15.0 3.2 %collective-permute-start.17 = (f32[256,384]{1,0:T(8,128)S(1)}, f32[256,384]{1,0:T(8,128)S(1)}, u32[]{:S(2)}, u32[]{:S(2)}) collective-permute-start(f32[256,384]{1,0:T(8,128)S(1)} %bitcast_multiply_fusion), channel_id=1, source_target_pairs={{0,1},{1,0},{2,3},{3,2},{4,5},{5,4},{6,7},{7,6},{8,9},{9,8},{10,11... | collective-permute-start | bytes 1179656 | tf_op jit(solution)/shard_map/ppermute | solution.py:32
  18.9 4.4 %collective-permute-done.14 = f32[256,384]{1,0:T(8,128)S(1)} collective-permute-done((f32[256,384]{1,0:T(8,128)S(1)}, f32[256,384]{1,0:T(8,128)S(1)}, u32[]{:S(2)}, u32[]{:S(2)}) %collective-permute-start.14) | collective-permute-done | bytes 393248 | tf_op jit(solution)/shard_map/ppermute | solution.py:28
  23.4 3.8 %collective-permute-start.16 = (f32[128,384]{1,0:T(8,128)S(1)}, f32[128,384]{1,0:T(8,128)S(1)}, u32[]{:S(2)}, u32[]{:S(2)}) collective-permute-start(f32[128,384]{1,0:T(8,128)S(1)} %get-tuple-element.36.rest_5_), channel_id=1, source_target_pairs={{0,6},{1,7},{2,0},{3,1},{4,2},{5,3},{6,4},{7,5},{8,14},{9,15},{10,... | collective-permute-start | bytes 589832 | tf_op jit(solution)/shard_map/ppermute | solution.py:28
  27.2 3.2 %collective-permute-start.20 = (f32[128,384]{1,0:T(8,128)S(1)}, f32[128,384]{1,0:T(8,128)S(1)}, u32[]{:S(2)}, u32[]{:S(2)}) collective-permute-start(f32[128,384]{1,0:T(8,128)S(1)} %get-tuple-element.37.rest_4_), channel_id=1, source_target_pairs={{0,1},{1,0},{2,3},{3,2},{4,5},{5,4},{6,7},{7,6},{8,9},{9,8},{10,11... | collective-permute-start | bytes 589832 | tf_op jit(solution)/shard_map/ppermute | solution.py:32
  32.9 3.2 %collective-permute-done.21.rest_13_ = f32[128,384]{1,0:T(8,128)S(1)} collective-permute-done((f32[128,384]{1,0:T(8,128)S(1)}, f32[128,384]{1,0:T(8,128)S(1)}, u32[]{:S(2)}, u32[]{:S(2)}) %collective-permute-start.21) | collective-permute-done | bytes 196640 | tf_op jit(solution)/shard_map/ppermute | solution.py:28
  41.8 4.2 %collective-permute-done.22.rest_14_ = f32[128,384]{1,0:T(8,128)S(1)} collective-permute-done((f32[128,384]{1,0:T(8,128)S(1)}, f32[128,384]{1,0:T(8,128)S(1)}, u32[]{:S(2)}, u32[]{:S(2)}) %collective-permute-start.22) | collective-permute-done | bytes 196640 | tf_op jit(solution)/shard_map/ppermute | solution.py:28
  48.8 4.6 %shard_map.78 = (f32[256,384]{1,0:T(8,128)}, f32[384,256]{1,0:T(8,128)}) custom-call(s32[9]{0:T(128)S(1)} %concatenate.25.ids, s32[1]{0:T(128)S(6)} %copy.19.live, f32[3072,384]{1,0:T(8,128)S(1)} %bitcast.60, f32[128,384]{1,0:T(8,128)S(1)} %get-tuple-element.41.rest_0_, f32[128,384]{1,0:T(8,128)S(1)} %get-tuple-element.40.rest_1_, ...), custom_call_target="tpu_custom_call" | custom-call | tf_op jit(solution)/shard_map/pallas_call | solution.py:160
  57.8 3.0 %collective-permute-start.28 = (f32[384,384]{1,0:T(8,128)S(1)}, f32[384,384]{1,0:T(8,128)}, u32[]{:S(2)}, u32[]{:S(2)}) collective-permute-start(f32[384,384]{1,0:T(8,128)S(1)} %bitcast.64), channel_id=1, source_target_pairs={{0,1},{1,0},{2,3},{3,2},{4,5},{5,4},{6,7},{7,6},{8,9},{9,8},{10,11... | collective-permute-start | bytes 1769480 | tf_op jit(solution)/shard_map/ppermute | solution.py:32
  62.8 4.5 %compare_select_fusion.3 = (s32[2048,1]{0,1:T(1,128)S(1)}, s32[2048,1]{0,1:T(1,128)S(1)}) fusion(s32[]{:T(128)} %bitcast.20, s32[]{:T(128)} %bitcast.21, s32[]{:T(128)} %bitcast.22, s32[]{:T(128)} %bitcast.23, s32[]{:T(128)} %bitcast.24, s32[]{:T(128)} %bitcast.26, s32[]{:T(128)} %bitcast.25, s32[1,2048]{1,0:T(1,128)S(1)} %copy-done.21), kind=kLoop, calls=%fused_computation.8 | loop fusion | flops 83968 | bytes 24604 | tf_op jit(solution)/shard_map/gather | solution.py:175
  68.0 6.7 %collective-permute-done = s32[2048]{0:T(1024)S(1)} collective-permute-done((s32[2048]{0:T(1024)S(1)}, s32[2048]{0:T(1024)S(1)}, u32[]{:S(2)}, u32[]{:S(2)}) %collective-permute-start) | collective-permute-done | bytes 8224 | tf_op jit(solution)/shard_map/ppermute | solution.py:36
  74.9 3.0 %collective-permute-start.27 = (f32[192,384]{1,0:T(8,128)S(1)}, f32[192,384]{1,0:T(8,128)S(1)}, u32[]{:S(2)}, u32[]{:S(2)}) collective-permute-start(f32[192,384]{1,0:T(8,128)S(1)} %get-tuple-element.14.rest_5_), channel_id=1, source_target_pairs={{0,6},{1,7},{2,0},{3,1},{4,2},{5,3},{6,4},{7,5},{8,14},{9,15},{10,... | collective-permute-start | bytes 884744 | tf_op jit(solution)/shard_map/ppermute | solution.py:28
  80.3 3.9 %gather_fusion.1 = f32[256,256]{1,0:T(8,128)} fusion(f32[4096,256]{1,0:T(8,128)} %all-gather.5.cloned.1.call-done, s32[1024]{0:T(1024)S(1)} %pad_clamp_fusion), kind=kCustom, calls=%fused_computation.1 | custom fusion | bytes 525312 | tf_op jit(solution)/shard_map/gather | solution.py:171
  88.5 3.2 %gather_fusion = f32[256,256]{1,0:T(8,128)S(1)} fusion(f32[4096,256]{1,0:T(8,128)} %all-gather.5.cloned.1.call-done, s32[1024]{0:T(1024)S(1)} %pad_clamp_fusion.1), kind=kCustom, calls=%fused_computation | custom fusion | bytes 525312 | tf_op jit(solution)/shard_map/gather | solution.py:170
  93.5 3.3 %collective-permute-start.6 = (f32[512,256]{1,0:T(8,128)S(1)}, f32[512,256]{1,0:T(8,128)S(1)}, u32[]{:S(2)}, u32[]{:S(2)}) collective-permute-start(f32[512,256]{1,0:T(8,128)S(1)} %constant_dynamic-update-slice_fusion), channel_id=1, source_target_pairs={{0,1},{1,0},{2,3},{3,2},{4,5},{5,4},{6,7},{7,6},{8,9},{9,8},{10,11... | collective-permute-start | bytes 1572872 | tf_op jit(solution)/shard_map/ppermute | solution.py:32
  97.9 3.0 %collective-permute-start.32 = (f32[192,384]{1,0:T(8,128)S(1)}, f32[192,384]{1,0:T(8,128)S(1)}, u32[]{:S(2)}, u32[]{:S(2)}) collective-permute-start(f32[192,384]{1,0:T(8,128)S(1)} %get-tuple-element.12.rest_9_), channel_id=1, source_target_pairs={{0,6},{1,7},{2,0},{3,1},{4,2},{5,3},{6,4},{7,5},{8,14},{9,15},{10,... | collective-permute-start | bytes 884744 | tf_op jit(solution)/shard_map/ppermute | solution.py:28
  100.9 3.2 %collective-permute-start.3 = (f32[512,256]{1,0:T(8,128)S(1)}, f32[512,256]{1,0:T(8,128)S(1)}, u32[]{:S(2)}, u32[]{:S(2)}) collective-permute-start(f32[512,256]{1,0:T(8,128)S(1)} %constant_dynamic-update-slice_fusion), channel_id=1, source_target_pairs={{0,6},{1,7},{2,0},{3,1},{4,2},{5,3},{6,4},{7,5},{8,14},{9,15},{10,... | collective-permute-start | bytes 1572872 | tf_op jit(solution)/shard_map/ppermute | solution.py:28
  104.3 4.1 %collective-permute-done.32.rest_13_ = f32[192,384]{1,0:T(8,128)S(1)} collective-permute-done((f32[192,384]{1,0:T(8,128)S(1)}, f32[192,384]{1,0:T(8,128)S(1)}, u32[]{:S(2)}, u32[]{:S(2)}) %collective-permute-start.32) | collective-permute-done | bytes 294944 | tf_op jit(solution)/shard_map/ppermute | solution.py:28
  108.4 3.7 %collective-permute-start.34 = (f32[192,384]{1,0:T(8,128)S(1)}, f32[192,384]{1,0:T(8,128)S(1)}, u32[]{:S(2)}, u32[]{:S(2)}) collective-permute-start(f32[192,384]{1,0:T(8,128)S(1)} %collective-permute-done.32.rest_13_), channel_id=1, source_target_pairs={{0,6},{1,7},{2,0},{3,1},{4,2},{5,3},{6,4},{7,5},{8,14},{9,15},{10,... | collective-permute-start | bytes 884744 | tf_op jit(solution)/shard_map/ppermute | solution.py:28
  114.1 5.5 %collective-permute-done.3 = f32[512,256]{1,0:T(8,128)S(1)} collective-permute-done((f32[512,256]{1,0:T(8,128)S(1)}, f32[512,256]{1,0:T(8,128)S(1)}, u32[]{:S(2)}, u32[]{:S(2)}) %collective-permute-start.3) | collective-permute-done | bytes 524320 | tf_op jit(solution)/shard_map/ppermute | solution.py:28
  119.6 3.7 %collective-permute-start.10 = (f32[256,256]{1,0:T(8,128)S(1)}, f32[256,256]{1,0:T(8,128)S(1)}, u32[]{:S(2)}, u32[]{:S(2)}) collective-permute-start(f32[256,256]{1,0:T(8,128)S(1)} %get-tuple-element.20.rest_9_), channel_id=1, source_target_pairs={{0,6},{1,7},{2,0},{3,1},{4,2},{5,3},{6,4},{7,5},{8,14},{9,15},{10,... | collective-permute-start | bytes 786440 | tf_op jit(solution)/shard_map/ppermute | solution.py:28
  125.9 3.7 %collective-permute-start.5 = (f32[256,256]{1,0:T(8,128)S(1)}, f32[256,256]{1,0:T(8,128)S(1)}, u32[]{:S(2)}, u32[]{:S(2)}) collective-permute-start(f32[256,256]{1,0:T(8,128)S(1)} %get-tuple-element.22.rest_5_), channel_id=1, source_target_pairs={{0,6},{1,7},{2,0},{3,1},{4,2},{5,3},{6,4},{7,5},{8,14},{9,15},{10,... | collective-permute-start | bytes 786440 | tf_op jit(solution)/shard_map/ppermute | solution.py:28
  130.4 5.5 %collective-permute-done.2 = f32[512,256]{1,0:T(8,128)S(1)} collective-permute-done((f32[512,256]{1,0:T(8,128)S(1)}, f32[512,256]{1,0:T(8,128)S(1)}, u32[]{:S(2)}, u32[]{:S(2)}) %collective-permute-start.2) | collective-permute-done | bytes 524320 | tf_op jit(solution)/shard_map/ppermute | solution.py:28
  136.5 3.1 %collective-permute-start.39 = (f32[384,256]{1,0:T(8,128)}, f32[384,256]{1,0:T(8,128)S(1)}, u32[]{:S(2)}, u32[]{:S(2)}) collective-permute-start(f32[384,256]{1,0:T(8,128)} %get-tuple-element.9), channel_id=1, source_target_pairs={{0,1},{1,0},{2,3},{3,2},{4,5},{5,4},{6,7},{7,6},{8,9},{9,8},{10,11... | collective-permute-start | bytes 1179656 | tf_op jit(solution)/shard_map/ppermute | solution.py:32
  146.8 4.5 %collective-permute-done.39 = f32[384,256]{1,0:T(8,128)S(1)} collective-permute-done((f32[384,256]{1,0:T(8,128)}, f32[384,256]{1,0:T(8,128)S(1)}, u32[]{:S(2)}, u32[]{:S(2)}) %collective-permute-start.39) | collective-permute-done | bytes 393248 | tf_op jit(solution)/shard_map/ppermute | solution.py:32
  155.0 3.8 %collective-permute-done.35 = f32[384,256]{1,0:T(8,128)S(1)} collective-permute-done((f32[384,256]{1,0:T(8,128)}, f32[384,256]{1,0:T(8,128)S(1)}, u32[]{:S(2)}, u32[]{:S(2)}) %collective-permute-start.35) | collective-permute-done | bytes 393248 | tf_op jit(solution)/shard_map/ppermute | solution.py:28
  159.6 3.3 %collective-permute-start.42 = (f32[192,256]{1,0:T(8,128)S(1)}, f32[192,256]{1,0:T(8,128)}, u32[]{:S(2)}, u32[]{:S(2)}) collective-permute-start(f32[192,256]{1,0:T(8,128)S(1)} %get-tuple-element.29.rest_20_), channel_id=1, source_target_pairs={{0,1},{1,0},{2,3},{3,2},{4,5},{5,4},{6,7},{7,6},{8,9},{9,8},{10,11... | collective-permute-start | bytes 589832 | tf_op jit(solution)/shard_map/ppermute | solution.py:32
  165.1 3.2 %collective-permute-start.45 = (f32[192,256]{1,0:T(8,128)}, f32[192,256]{1,0:T(8,128)}, u32[]{:S(2)}, u32[]{:S(2)}) collective-permute-start(f32[192,256]{1,0:T(8,128)} %collective-permute-done.43.rest_29_), channel_id=1, source_target_pairs={{0,6},{1,7},{2,0},{3,1},{4,2},{5,3},{6,4},{7,5},{8,14},{9,15},{10,... | collective-permute-start | bytes 589832 | tf_op jit(solution)/shard_map/ppermute | solution.py:28
  170.5 10.8 %shard_map.77 = (bf16[256,2048]{1,0:T(8,128)(2,1)S(1)}, bf16[256,2048]{1,0:T(8,128)(2,1)S(1)}) custom-call(s32[1,2048]{1,0:T(1,128)S(1)} %fusion.place, f32[256,256]{1,0:T(8,128)S(1)} %gather_fusion, f32[256,256]{1,0:T(8,128)S(1)} %collective-permute-done.1.rest_1_, f32[256,256]{1,0:T(8,128)S(1)} %get-tuple-element.25.rest_2_, ...), custom_call_target="tpu_custom_call" | custom-call | tf_op jit(solution)/shard_map/pallas_call | solution.py:176
  187.6 3.2 %shard_map.79.coupling = f32[256,384]{1,0:T(8,128)} custom-call(s32[9]{0:T(128)S(1)} %concatenate.25.ids, s32[1]{0:T(128)S(6)} %copy.19.live, bf16[256,2048]{1,0:T(8,128)(2,1)S(1)} %copy-done.3, bf16[256,2048]{1,0:T(8,128)(2,1)S(1)} %copy-done.5, f32[2048,384]{1,0:T(8,128)S(1)} %copy-done.1), custom_call_target="tpu_custom_call" | custom-call | tf_op jit(solution)/shard_map/pallas_call | solution.py:186
  192.8 11.4 %shard_map.80 = f32[3072,384]{1,0:T(8,128)} custom-call(s32[9]{0:T(128)S(1)} %concatenate.25.ids, f32[384,384]{1,0:T(8,128)} %bitcast.61, f32[256,384]{1,0:T(8,128)} %shard_map.79.coupling, f32[192,384]{1,0:T(8,128)S(1)} %get-tuple-element.19.rest_0_, f32[192,384]{1,0:T(8,128)S(1)} %get-tuple-element.18.rest_1_, f32[192,384]{1,0:T(8,128)S(1)} %get-tuple-element.17.rest_2_, ...), custom_call_target="tpu_custom_call" | custom-call | tf_op jit(solution)/shard_map/pallas_call | solution.py:196
  204.2 39.3 %reduce-scatter.2.cloned.1.call-done = f32[384,384]{1,0:T(8,128)} async-done(((f32[3072,384]{1,0:T(8,128)}), f32[384,384]{1,0:T(8,128)}) %reduce-scatter.2.cloned.1.call-update) | async-done | bytes 589840 | tf_op jit(solution)/shard_map/reduce_scatter | solution.py:203
  (161 shorter events, 62.1 us)
Async XLA Ops:
  7.2 39.3 %all-gather.9.cloned.1.call-start = ((), (), s32[]{:S(2)}) async-start(), calls=%async_computation.4 | async-start | bytes 5308416 | tf_op jit(solution)/shard_map/all_gather | solution.py:154
  7.9 72.4 %all-gather.5.cloned.1.call-start = ((), (), s32[]{:S(2)}) async-start(), calls=%async_computation.1 | async-start | bytes 4718592 | tf_op jit(solution)/shard_map/all_gather | solution.py:153
  8.6 174.6 %all-gather.7.cloned.1.call-start = ((), (), s32[]{:S(2)}) async-start(), calls=%async_computation.2 | async-start | bytes 3538944 | tf_op jit(solution)/shard_map/all_gather | solution.py:185
  15.0 15.4 %collective-permute-start.17 = (f32[256,384]{1,0:T(8,128)S(1)}, f32[256,384]{1,0:T(8,128)S(1)}, u32[]{:S(2)}, u32[]{:S(2)}) collective-permute-start(f32[256,384]{1,0:T(8,128)S(1)} %bitcast_multiply_fusion), channel_id=1, source_target_pairs={{0,1},{1,0},{2,3},{3,2},{4,5},{5,4},{6,7},{7,6},{8,9},{9,8},{10,11... | collective-permute-start | bytes 1179656 | tf_op jit(solution)/shard_map/ppermute | solution.py:32
  18.2 14.3 %collective-permute-start.13 = (f32[256,384]{1,0:T(8,128)S(1)}, f32[256,384]{1,0:T(8,128)S(1)}, u32[]{:S(2)}, u32[]{:S(2)}) collective-permute-start(f32[256,384]{1,0:T(8,128)S(1)} %bitcast_multiply_fusion), channel_id=1, source_target_pairs={{0,2},{1,3},{2,4},{3,5},{4,6},{5,7},{6,0},{7,1},{8,10},{9,11},{10,... | collective-permute-start | bytes 1179656 | tf_op jit(solution)/shard_map/ppermute | solution.py:28
  53.4 190.0 %reduce-scatter.2.cloned.1.call-start = ((), (), s32[]{:S(2)}) async-start(), calls=%async_computation.3 | async-start | bytes 5308416 | tf_op jit(solution)/shard_map/reduce_scatter | solution.py:203
  54.7 20.1 %collective-permute-start.25 = (f32[384,384]{1,0:T(8,128)S(1)}, f32[384,384]{1,0:T(8,128)S(1)}, u32[]{:S(2)}, u32[]{:S(2)}) collective-permute-start(f32[384,384]{1,0:T(8,128)S(1)} %bitcast.62), channel_id=1, source_target_pairs={{0,6},{1,7},{2,0},{3,1},{4,2},{5,3},{6,4},{7,5},{8,14},{9,15},{10,... | collective-permute-start | bytes 1769480 | tf_op jit(solution)/shard_map/ppermute | solution.py:28
  57.8 27.9 %collective-permute-start.24 = (f32[384,384]{1,0:T(8,128)S(1)}, f32[384,384]{1,0:T(8,128)S(1)}, u32[]{:S(2)}, u32[]{:S(2)}) collective-permute-start(f32[384,384]{1,0:T(8,128)S(1)} %bitcast.63), channel_id=1, source_target_pairs={{0,2},{1,3},{2,4},{3,5},{4,6},{5,7},{6,0},{7,1},{8,10},{9,11},{10,... | collective-permute-start | bytes 1769480 | tf_op jit(solution)/shard_map/ppermute | solution.py:28
  57.8 39.0 %collective-permute-start.28 = (f32[384,384]{1,0:T(8,128)S(1)}, f32[384,384]{1,0:T(8,128)}, u32[]{:S(2)}, u32[]{:S(2)}) collective-permute-start(f32[384,384]{1,0:T(8,128)S(1)} %bitcast.64), channel_id=1, source_target_pairs={{0,1},{1,0},{2,3},{3,2},{4,5},{5,4},{6,7},{7,6},{8,9},{9,8},{10,11... | collective-permute-start | bytes 1769480 | tf_op jit(solution)/shard_map/ppermute | solution.py:32
  60.8 13.9 %collective-permute-start = (s32[2048]{0:T(1024)S(1)}, s32[2048]{0:T(1024)S(1)}, u32[]{:S(2)}, u32[]{:S(2)}) collective-permute-start(s32[2048]{0:T(1024)S(1)} %bitcast.68), channel_id=1, source_target_pairs={{0,64},{64,0},{1,65},{65,1},{2,66},{66,2},{3,67},{67,3},{4,68},{68... | collective-permute-start | bytes 24584 | tf_op jit(solution)/shard_map/ppermute | solution.py:36
  74.9 26.0 %collective-permute-start.27 = (f32[192,384]{1,0:T(8,128)S(1)}, f32[192,384]{1,0:T(8,128)S(1)}, u32[]{:S(2)}, u32[]{:S(2)}) collective-permute-start(f32[192,384]{1,0:T(8,128)S(1)} %get-tuple-element.14.rest_5_), channel_id=1, source_target_pairs={{0,6},{1,7},{2,0},{3,1},{4,2},{5,3},{6,4},{7,5},{8,14},{9,15},{10,... | collective-permute-start | bytes 884744 | tf_op jit(solution)/shard_map/ppermute | solution.py:28
  77.9 23.0 %collective-permute-start.31 = (f32[192,384]{1,0:T(8,128)S(1)}, f32[192,384]{1,0:T(8,128)S(1)}, u32[]{:S(2)}, u32[]{:S(2)}) collective-permute-start(f32[192,384]{1,0:T(8,128)S(1)} %get-tuple-element.15.rest_4_), channel_id=1, source_target_pairs={{0,1},{1,0},{2,3},{3,2},{4,5},{5,4},{6,7},{7,6},{8,9},{9,8},{10,11... | collective-permute-start | bytes 884744 | tf_op jit(solution)/shard_map/ppermute | solution.py:32
  85.7 18.5 %collective-permute-start.30 = (f32[192,384]{1,0:T(8,128)S(1)}, f32[192,384]{1,0:T(8,128)}, u32[]{:S(2)}, u32[]{:S(2)}) collective-permute-start(f32[192,384]{1,0:T(8,128)S(1)} %get-tuple-element.16.rest_3_), channel_id=1, source_target_pairs={{0,1},{1,0},{2,3},{3,2},{4,5},{5,4},{6,7},{7,6},{8,9},{9,8},{10,11... | collective-permute-start | bytes 884744 | tf_op jit(solution)/shard_map/ppermute | solution.py:32
  93.5 19.0 %collective-permute-start.6 = (f32[512,256]{1,0:T(8,128)S(1)}, f32[512,256]{1,0:T(8,128)S(1)}, u32[]{:S(2)}, u32[]{:S(2)}) collective-permute-start(f32[512,256]{1,0:T(8,128)S(1)} %constant_dynamic-update-slice_fusion), channel_id=1, source_target_pairs={{0,1},{1,0},{2,3},{3,2},{4,5},{5,4},{6,7},{7,6},{8,9},{9,8},{10,11... | collective-permute-start | bytes 1572872 | tf_op jit(solution)/shard_map/ppermute | solution.py:32
  100.9 18.7 %collective-permute-start.3 = (f32[512,256]{1,0:T(8,128)S(1)}, f32[512,256]{1,0:T(8,128)S(1)}, u32[]{:S(2)}, u32[]{:S(2)}) collective-permute-start(f32[512,256]{1,0:T(8,128)S(1)} %constant_dynamic-update-slice_fusion), channel_id=1, source_target_pairs={{0,6},{1,7},{2,0},{3,1},{4,2},{5,3},{6,4},{7,5},{8,14},{9,15},{10,... | collective-permute-start | bytes 1572872 | tf_op jit(solution)/shard_map/ppermute | solution.py:28
  104.2 19.1 %collective-permute-start.26 = (f32[192,384]{1,0:T(8,128)S(1)}, f32[192,384]{1,0:T(8,128)S(1)}, u32[]{:S(2)}, u32[]{:S(2)}) collective-permute-start(f32[192,384]{1,0:T(8,128)S(1)} %get-tuple-element.17.rest_2_), channel_id=1, source_target_pairs={{0,2},{1,3},{2,4},{3,5},{4,6},{5,7},{6,0},{7,1},{8,10},{9,11},{10,... | collective-permute-start | bytes 884744 | tf_op jit(solution)/shard_map/ppermute | solution.py:28
  108.4 17.6 %collective-permute-start.34 = (f32[192,384]{1,0:T(8,128)S(1)}, f32[192,384]{1,0:T(8,128)S(1)}, u32[]{:S(2)}, u32[]{:S(2)}) collective-permute-start(f32[192,384]{1,0:T(8,128)S(1)} %collective-permute-done.32.rest_13_), channel_id=1, source_target_pairs={{0,6},{1,7},{2,0},{3,1},{4,2},{5,3},{6,4},{7,5},{8,14},{9,15},{10,... | collective-permute-start | bytes 884744 | tf_op jit(solution)/shard_map/ppermute | solution.py:28
  112.1 17.6 %collective-permute-start.33 = (f32[192,384]{1,0:T(8,128)S(1)}, f32[192,384]{1,0:T(8,128)S(1)}, u32[]{:S(2)}, u32[]{:S(2)}) collective-permute-start(f32[192,384]{1,0:T(8,128)S(1)} %collective-permute-done.29.rest_10_), channel_id=1, source_target_pairs={{0,2},{1,3},{2,4},{3,5},{4,6},{5,7},{6,0},{7,1},{8,10},{9,11},{10,... | collective-permute-start | bytes 884744 | tf_op jit(solution)/shard_map/ppermute | solution.py:28
  112.5 23.4 %collective-permute-start.2 = (f32[512,256]{1,0:T(8,128)S(1)}, f32[512,256]{1,0:T(8,128)S(1)}, u32[]{:S(2)}, u32[]{:S(2)}) collective-permute-start(f32[512,256]{1,0:T(8,128)S(1)} %constant_dynamic-update-slice_fusion), channel_id=1, source_target_pairs={{0,2},{1,3},{2,4},{3,5},{4,6},{5,7},{6,0},{7,1},{8,10},{9,11},{10,... | collective-permute-start | bytes 1572872 | tf_op jit(solution)/shard_map/ppermute | solution.py:28
  119.6 16.9 %collective-permute-start.10 = (f32[256,256]{1,0:T(8,128)S(1)}, f32[256,256]{1,0:T(8,128)S(1)}, u32[]{:S(2)}, u32[]{:S(2)}) collective-permute-start(f32[256,256]{1,0:T(8,128)S(1)} %get-tuple-element.20.rest_9_), channel_id=1, source_target_pairs={{0,6},{1,7},{2,0},{3,1},{4,2},{5,3},{6,4},{7,5},{8,14},{9,15},{10,... | collective-permute-start | bytes 786440 | tf_op jit(solution)/shard_map/ppermute | solution.py:28
  124.1 15.5 %collective-permute-start.7 = (f32[256,256]{1,0:T(8,128)S(1)}, f32[256,256]{1,0:T(8,128)S(1)}, u32[]{:S(2)}, u32[]{:S(2)}) collective-permute-start(f32[256,256]{1,0:T(8,128)S(1)} %get-tuple-element.21.rest_8_), channel_id=1, source_target_pairs={{0,2},{1,3},{2,4},{3,5},{4,6},{5,7},{6,0},{7,1},{8,10},{9,11},{10,... | collective-permute-start | bytes 786440 | tf_op jit(solution)/shard_map/ppermute | solution.py:28
  125.9 14.3 %collective-permute-start.5 = (f32[256,256]{1,0:T(8,128)S(1)}, f32[256,256]{1,0:T(8,128)S(1)}, u32[]{:S(2)}, u32[]{:S(2)}) collective-permute-start(f32[256,256]{1,0:T(8,128)S(1)} %get-tuple-element.22.rest_5_), channel_id=1, source_target_pairs={{0,6},{1,7},{2,0},{3,1},{4,2},{5,3},{6,4},{7,5},{8,14},{9,15},{10,... | collective-permute-start | bytes 786440 | tf_op jit(solution)/shard_map/ppermute | solution.py:28
  129.6 13.5 %collective-permute-start.36 = (f32[384,256]{1,0:T(8,128)}, f32[384,256]{1,0:T(8,128)S(1)}, u32[]{:S(2)}, u32[]{:S(2)}) collective-permute-start(f32[384,256]{1,0:T(8,128)} %get-tuple-element.9), channel_id=1, source_target_pairs={{0,6},{1,7},{2,0},{3,1},{4,2},{5,3},{6,4},{7,5},{8,14},{9,15},{10,... | collective-permute-start | bytes 1179656 | tf_op jit(solution)/shard_map/ppermute | solution.py:28
  136.5 14.9 %collective-permute-start.39 = (f32[384,256]{1,0:T(8,128)}, f32[384,256]{1,0:T(8,128)S(1)}, u32[]{:S(2)}, u32[]{:S(2)}) collective-permute-start(f32[384,256]{1,0:T(8,128)} %get-tuple-element.9), channel_id=1, source_target_pairs={{0,1},{1,0},{2,3},{3,2},{4,5},{5,4},{6,7},{7,6},{8,9},{9,8},{10,11... | collective-permute-start | bytes 1179656 | tf_op jit(solution)/shard_map/ppermute | solution.py:32
  139.6 14.6 %collective-permute-start.8 = (f32[256,256]{1,0:T(8,128)S(1)}, f32[256,256]{1,0:T(8,128)S(1)}, u32[]{:S(2)}, u32[]{:S(2)}) collective-permute-start(f32[256,256]{1,0:T(8,128)S(1)} %get-tuple-element.24.rest_3_), channel_id=1, source_target_pairs={{0,1},{1,0},{2,3},{3,2},{4,5},{5,4},{6,7},{7,6},{8,9},{9,8},{10,11... | collective-permute-start | bytes 786440 | tf_op jit(solution)/shard_map/ppermute | solution.py:32
  140.2 14.5 %collective-permute-start.4 = (f32[256,256]{1,0:T(8,128)S(1)}, f32[256,256]{1,0:T(8,128)S(1)}, u32[]{:S(2)}, u32[]{:S(2)}) collective-permute-start(f32[256,256]{1,0:T(8,128)S(1)} %get-tuple-element.25.rest_2_), channel_id=1, source_target_pairs={{0,2},{1,3},{2,4},{3,5},{4,6},{5,7},{6,0},{7,1},{8,10},{9,11},{10,... | collective-permute-start | bytes 786440 | tf_op jit(solution)/shard_map/ppermute | solution.py:28
  143.1 15.6 %collective-permute-start.35 = (f32[384,256]{1,0:T(8,128)}, f32[384,256]{1,0:T(8,128)S(1)}, u32[]{:S(2)}, u32[]{:S(2)}) collective-permute-start(f32[384,256]{1,0:T(8,128)} %get-tuple-element.9), channel_id=1, source_target_pairs={{0,2},{1,3},{2,4},{3,5},{4,6},{5,7},{6,0},{7,1},{8,10},{9,11},{10,... | collective-permute-start | bytes 1179656 | tf_op jit(solution)/shard_map/ppermute | solution.py:28
  159.6 31.2 %collective-permute-start.42 = (f32[192,256]{1,0:T(8,128)S(1)}, f32[192,256]{1,0:T(8,128)}, u32[]{:S(2)}, u32[]{:S(2)}) collective-permute-start(f32[192,256]{1,0:T(8,128)S(1)} %get-tuple-element.29.rest_20_), channel_id=1, source_target_pairs={{0,1},{1,0},{2,3},{3,2},{4,5},{5,4},{6,7},{7,6},{8,9},{9,8},{10,11... | collective-permute-start | bytes 589832 | tf_op jit(solution)/shard_map/ppermute | solution.py:32
  164.4 26.4 %collective-permute-start.41 = (f32[192,256]{1,0:T(8,128)}, f32[192,256]{1,0:T(8,128)}, u32[]{:S(2)}, u32[]{:S(2)}) collective-permute-start(f32[192,256]{1,0:T(8,128)} %get-tuple-element.30.rest_19_), channel_id=1, source_target_pairs={{0,1},{1,0},{2,3},{3,2},{4,5},{5,4},{6,7},{7,6},{8,9},{9,8},{10,11... | collective-permute-start | bytes 589832 | tf_op jit(solution)/shard_map/ppermute | solution.py:32
  165.1 25.7 %collective-permute-start.37 = (f32[192,256]{1,0:T(8,128)}, f32[192,256]{1,0:T(8,128)}, u32[]{:S(2)}, u32[]{:S(2)}) collective-permute-start(f32[192,256]{1,0:T(8,128)} %get-tuple-element.31.rest_18_), channel_id=1, source_target_pairs={{0,2},{1,3},{2,4},{3,5},{4,6},{5,7},{6,0},{7,1},{8,10},{9,11},{10,... | collective-permute-start | bytes 589832 | tf_op jit(solution)/shard_map/ppermute | solution.py:28
  165.1 25.7 %collective-permute-start.45 = (f32[192,256]{1,0:T(8,128)}, f32[192,256]{1,0:T(8,128)}, u32[]{:S(2)}, u32[]{:S(2)}) collective-permute-start(f32[192,256]{1,0:T(8,128)} %collective-permute-done.43.rest_29_), channel_id=1, source_target_pairs={{0,6},{1,7},{2,0},{3,1},{4,2},{5,3},{6,4},{7,5},{8,14},{9,15},{10,... | collective-permute-start | bytes 589832 | tf_op jit(solution)/shard_map/ppermute | solution.py:28
  168.7 22.1 %collective-permute-start.44 = (f32[192,256]{1,0:T(8,128)}, f32[192,256]{1,0:T(8,128)}, u32[]{:S(2)}, u32[]{:S(2)}) collective-permute-start(f32[192,256]{1,0:T(8,128)} %collective-permute-done.40.rest_26_), channel_id=1, source_target_pairs={{0,2},{1,3},{2,4},{3,5},{4,6},{5,7},{6,0},{7,1},{8,10},{9,11},{10,... | collective-permute-start | bytes 589832 | tf_op jit(solution)/shard_map/ppermute | solution.py:28
  (40 other events, 348.6 us)
Sparse Core Ops, SparseCore 0:
  9.7 36.7 all-gather.8
  48.2 32.0 all-gather.4
  82.6 27.6 all-gather.6
  204.3 39.0 reduce-scatter.1

commit v2 on v0

v2 whole, which is shorter than its diff:
```python
import functools

import jax
import jax.numpy as jnp
from jax import lax
from jax.experimental import pallas as pl
from jax.experimental.pallas import tpu as pltpu
from jax.sharding import PartitionSpec as P

ROOT = 4096
SEP = 3072
ANC = 2048
TILE = 128
SIDE = 8
BAND = ANC // SIDE
WIDE = SEP // SIDE
KEEP = ROOT // (2 * SIDE)

f32 = jnp.float32
bf16 = jnp.bfloat16
VMEM = pl.BlockSpec(memory_space=pltpu.VMEM)
SMEM = pl.BlockSpec(memory_space=pltpu.SMEM)
ANY = pl.BlockSpec(memory_space=pl.ANY)


def hold(arrays, deps):
    n = len(arrays)
    return pl.pallas_call(
        lambda *refs: None,
        out_shape=[jax.ShapeDtypeStruct(x.shape, x.dtype) for x in arrays],
        in_specs=[ANY] * (n + len(deps)),
        out_specs=[ANY] * n,
        input_output_aliases={i: i for i in range(n)},
        compiler_params=pltpu.CompilerParams(vmem_limit_bytes=60 * 2**20),
    )(*arrays, *deps)


def shift(x, axis, step):
    return lax.ppermute(x, axis, [(i, (i // 2 + step) % 4 * 2 + i % 2) for i in range(SIDE)])


def swap(x, axis):
    return lax.ppermute(x, axis, [(i, i ^ 1) for i in range(SIDE)])


def swap_group(x):
    return lax.ppermute(x, "grp", [(0, 1), (1, 0)])


ORDER = ((0, 0), (-1, 0), (1, 0), (2, 0), (0, 1), (-1, 1), (1, 1), (2, 1))


def near_col(x):
    return [x, shift(x, "col", 1), shift(x, "col", -1), shift(x, "col", 2), swap(x, "col")]


def rest_col(far, other):
    return [shift(other, "col", 1), shift(other, "col", -1), swap(far, "col")]


def gather_col(x, meanwhile=()):
    *near, far, other = near_col(x)
    far, other, *rest = hold([far, other, *meanwhile], near[1:])
    return [*near, far, other, *rest_col(far, other)], rest


def fetch(refs, buffer, sems):
    copies = [pltpu.make_async_copy(ref, buffer.at[p], sems.at[p]) for p, ref in enumerate(refs)]
    for copy in copies:
        copy.start()
    return copies


def ids_of(axis):
    i = lax.axis_index(axis)
    return jnp.stack([(i // 2 + ring) % 4 * 2 + jnp.bitwise_xor(i % 2, pair) for ring, pair in ORDER]).astype(jnp.int32)


def place_of(block, axis):
    i = lax.axis_index(axis)
    ring = (block // 2 - i // 2) % 4
    first = jnp.where(ring == 3, 1, jnp.where(ring == 0, 0, ring + 1))
    return first + 4 * jnp.bitwise_xor(block % 2, i % 2)


def split(x):
    high = x.astype(bf16)
    return high, (x - high.astype(f32)).astype(bf16)


def dot(a, b):
    return jnp.dot(a, b, preferred_element_type=f32)


def dot3(a, b):
    return dot(a[0], b[0]) + (dot(a[0], b[1]) + dot(a[1], b[0]))


def call(kernel, out, scalars, blocks, arrays, scratch, copies, work):
    return pl.pallas_call(
        kernel,
        out_shape=out,
        in_specs=[SMEM] * len(scalars) + [VMEM] * len(blocks) + [ANY] * len(arrays),
        out_specs=jax.tree.map(lambda _: VMEM, out),
        scratch_shapes=[pltpu.VMEM(s, d) for s, d in scratch] + [pltpu.SemaphoreType.DMA((copies,))],
        compiler_params=pltpu.CompilerParams(vmem_limit_bytes=60 * 2**20),
        cost_estimate=pl.CostEstimate(flops=work * 10**9, bytes_accessed=work * 3 * 10**6, transcendentals=0),
    )(*scalars, *blocks, *arrays)


def array(*shape, dtype=f32):
    return jax.ShapeDtypeStruct(shape, dtype)


def update_sum(cols, below, diag, below_buf, diag_buf, sems):
    n = len(below)
    below_in = fetch(below, below_buf, sems)
    diag_in = [
        pltpu.make_async_copy(
            diag.at[pl.ds(pl.multiple_of(cols[p] * WIDE, WIDE), WIDE)], diag_buf.at[p], sems.at[n + p]
        )
        for p in range(n)
    ]
    for copy in diag_in:
        copy.start()
    total = jnp.zeros((BAND, WIDE), f32)
    for p in range(n):
        below_in[p].wait()
        diag_in[p].wait()
        total += dot3(split(below_buf[p]), split(diag_buf[p]))
    return total


def update_near_kernel(cols, *rest):
    out, *scratch = rest[6:]
    out[...] = update_sum(cols, rest[:5], rest[5], *scratch)


def update_kernel(cols, row, live, part, *rest):
    flipped, *scratch = rest[4:]
    total = part[...] + update_sum(cols, rest[:3], rest[3], *scratch)
    ids = row[0] * BAND + lax.broadcasted_iota(jnp.int32, (BAND, WIDE), 0)
    flipped[...] = jnp.where(ids < live[0], total, 0.0).T


def pick_rows(place, source, out, first, count):
    step = 32

    def body(j, carry):
        at = pl.multiple_of(j * step, step)
        for i in range(0, step, 8):
            found = [source[pl.ds(place[first + at + i + k], 1), :] for k in range(8)]
            out[pl.ds(at + i, 8), :] = jnp.concatenate(found, axis=0)
        return carry

    lax.fori_loop(0, count // step, body, 0)


def root_rows_kernel(place, root, _, own, other, source, found, sems):
    copy = pltpu.make_async_copy(root, source, sems.at[0])
    copy.start()
    copy.wait()
    for half, out in enumerate((own, other)):
        pick_rows(place, source, found, half * BAND, BAND)
        out[...] = found[...].T


def coupling_kernel(place, row, live, *rest):
    update, pieces, out, update_buf, source, found, sems = rest[0], rest[1:9], *rest[9:]
    update_in = [
        pltpu.make_async_copy(update.at[pl.ds(p * WIDE, WIDE)], update_buf.at[p], sems.at[8 + p]) for p in range(8)
    ]
    pieces_in = [
        pltpu.make_async_copy(pieces[p], source.at[pl.ds(p * 2 * KEEP, 2 * KEEP)], sems.at[p]) for p in range(8)
    ]
    for copy in pieces_in + update_in:
        copy.start()
    for copy in pieces_in:
        copy.wait()
    total = jnp.zeros((WIDE, BAND), f32)
    for p in range(8):
        pick_rows(place, source, found, p * BAND, BAND)
        update_in[p].wait()
        total += dot3(split(update_buf[p]), split(found[...]))
    ids = row[0] * BAND + lax.broadcasted_iota(jnp.int32, (BAND, WIDE), 0)
    out[...] = jnp.where(ids < live[0], -total.T, 0.0)


def gram_kernel(diag, *rest):
    pieces, out, buffer, sems = rest[:8], *rest[9:]
    copies = fetch(pieces, buffer, sems)
    right = split(diag[...])
    for p in range(8):
        copies[p].wait()
        out[p] = dot3(split(buffer[p].T), right)


def partial_kernel(first, count, cols, coupling, *rest):
    update, gram, out, update_buf, gram_buf, out_buf, sems = rest[:count], rest[count], *rest[-5:]
    update_in = fetch(update, update_buf, sems)
    gram_in = [
        pltpu.make_async_copy(gram.at[first + p], gram_buf.at[p], sems.at[count + p]) for p in range(count)
    ]
    for copy in gram_in:
        copy.start()
    right = split(-coupling[...])
    sent = []
    for p in range(count):
        update_in[p].wait()
        gram_in[p].wait()
        out_buf[p] = gram_buf[p] + dot3(split(update_buf[p]), right)
        at = pl.ds(pl.multiple_of(cols[first + p] * WIDE, WIDE), WIDE)
        sent.append(pltpu.make_async_copy(out_buf.at[p], out.at[at], sems.at[2 * count + p]))
        sent[-1].start()
    for copy in sent:
        copy.wait()


def partial(first, update, cols, coupling, gram, onto=None):
    count = len(update)
    given = [cols, coupling, *update, gram] + ([] if onto is None else [onto])
    return pl.pallas_call(
        functools.partial(partial_kernel, first, count),
        out_shape=array(SEP, WIDE),
        in_specs=[SMEM, VMEM] + [ANY] * (len(given) - 2),
        out_specs=ANY,
        scratch_shapes=[
            pltpu.VMEM((count, WIDE, BAND), f32),
            pltpu.VMEM((count, WIDE, WIDE), f32),
            pltpu.VMEM((count, WIDE, WIDE), f32),
            pltpu.SemaphoreType.DMA((3 * count,)),
        ],
        input_output_aliases={} if onto is None else {len(given) - 1: 0},
        compiler_params=pltpu.CompilerParams(vmem_limit_bytes=60 * 2**20),
        cost_estimate=pl.CostEstimate(flops=count * 10**9, bytes_accessed=count * 3 * 10**6, transcendentals=0),
    )(*given)


def per_device(root_inverse, ancestor_map, live_rows, factor_below, diag_inverse, tile_mask):
    row, group = lax.axis_index("row"), lax.axis_index("grp")
    cols = ids_of("col")
    diag_block = diag_inverse[0]
    own_map = ancestor_map[0]
    other_map = swap_group(own_map)

    root_cols = lax.all_gather(root_inverse, "row", axis=0, tiled=True)

    diag_cols = lax.all_gather(diag_block, "row", axis=0, tiled=True)

    diag_all = near_col(diag_block)
    diag_all += rest_col(*diag_all[3:])
    tile_keep = jnp.repeat(jnp.repeat(tile_mask[0], TILE, axis=0), TILE, axis=1).astype(f32)
    below, other_map = hold([factor_below[0] * tile_keep, other_map[None]], diag_all)

    gram = call(
        gram_kernel, array(SIDE, WIDE, WIDE), [], [diag_block], diag_all + [below], [((SIDE, WIDE, WIDE), f32)], 8, 12
    )
    place = jnp.concatenate([lax.dynamic_slice_in_dim(m, row * BAND, BAND) for m in (own_map, other_map[0])])
    own_rows, other_rows = call(
        root_rows_kernel, (array(KEEP, BAND), array(KEEP, BAND)), [place], [], [root_cols, below],
        [((ROOT, KEEP), f32), ((BAND, KEEP), f32)], 1, 5,
    )
    below_near = near_col(below)
    *below_near, gram, other_rows = hold([*below_near, gram, swap_group(other_rows)], [])
    below_rest = rest_col(*below_near[3:])
    part = call(
        update_near_kernel, array(BAND, WIDE), [cols[:5]], [], below_near + [diag_cols],
        [((5, BAND, WIDE), f32), ((5, WIDE, WIDE), f32)], 10, 5,
    )
    picked = jnp.concatenate([own_rows, other_rows], axis=0)
    picked, part = hold([picked, part], below_rest)

    flipped = call(
        update_kernel, array(WIDE, BAND), [cols[5:], row[None], live_rows], [part], below_rest + [diag_cols],
        [((3, BAND, WIDE), f32), ((3, WIDE, WIDE), f32)], 6, 3,
    )
    update_rows = lax.all_gather(flipped, "row", axis=0, tiled=True)
    picked_all = near_col(picked)
    picked_all += rest_col(*picked_all[3:])
    flipped, gram = hold([flipped, gram], picked_all)

    half = (own_map // (ROOT // 2) != group).astype(jnp.int32)
    place = place_of(own_map % (ROOT // 2) // KEEP, "col") * (2 * KEEP) + half * KEEP + own_map % KEEP
    coupling = call(
        coupling_kernel, array(BAND, WIDE), [place, row[None], live_rows], [], [update_rows] + picked_all,
        [((SIDE, WIDE, BAND), f32), ((ROOT, BAND), f32), ((BAND, BAND), f32)], 16, 12,
    )
    update_near = near_col(flipped)
    update_near = hold(update_near, [coupling])
    update_rest = rest_col(*update_near[3:])
    total = partial(0, update_near, cols, coupling, gram)
    (total,) = hold([total], update_rest)
    total = partial(5, update_rest, cols, coupling, gram, total)
    separator = lax.psum_scatter(total, "row", scatter_dimension=0, tiled=True)
    return (coupling[None], separator[None])


def solution(mesh):
    return jax.shard_map(
        per_device,
        mesh=mesh,
        in_specs=(
            P("row", ("grp", "col")),
            P("grp", None),
            P("grp"),
            P("grp", "row", "col"),
            P("grp", "row", "col"),
            P("grp", "row", "col"),
        ),
        out_specs=(P("grp", "row", "col"), P("grp", "row", "col")),
        check_vma=False,
    )
```

time: 650 us -> 227 us (0.35)
  waiting for transfers between devices: 539 us -> 95.4 us
  matrix products: 54 us -> 0 us
  starting transfers between devices: 0.54 us -> 52.1 us
  Pallas kernels: 0 us -> 49.2 us
  other arithmetic: 19.5 us -> 5.99 us
  local copies, waits for them, and re-layouts: 21.8 us -> 9.04 us
    all_gather x7 -> x3, waiting for transfers between devices: 466 us -> 0.02 us  [the longest x1 0.02 us: per_device(): update_rows = lax.all_gather(flipped, 'row', axis=0, tiled=True)]
    psum x1 -> x0, waiting for transfers between devices: 70.5 us -> none  [per_device(): summed = lax.psum(gram - cross, 'row')]
    ppermute x0 -> x30, waiting for transfers between devices: none -> 55.2 us  [the longest x20 40.7 us: shift(): lax.ppermute(x, axis, [(i, (i // 2 + step) % 4 * 2 + i % 2) for i in rang...]
    dot_general x4 -> x0, matrix products: 54 us -> none  [the longest x1 24 us: per_device(): jnp.dot(lax.all_gather(root_inverse, ('grp', 'col'), axis=1, tiled=True),...]
    ppermute x0 -> x30, starting transfers between devices: none -> 52 us  [the longest x20 32.8 us: shift(): lax.ppermute(x, axis, [(i, (i // 2 + step) % 4 * 2 + i % 2) for i in rang...]
    pallas_call x0 -> x13, Pallas kernels: none -> 49.2 us  [the longest x5 38.4 us: call(): pl.pallas_call(kernel, out_shape=out, in_specs=[SMEM] * len(scalars) + [V...]
    reduce_scatter x0 -> x1, waiting for transfers between devices: none -> 38.8 us  [per_device(): separator = lax.psum_scatter(total, 'row', scatter_dimension=0, tiled=True)]
    scatter-add x1 -> x0, other arithmetic: 16.2 us -> none  [per_device(): jnp.zeros((ROOT, col_width), jnp.float32).at[ancestor_ids].add(panel)]
  transfers between devices with their start and end apart: 8 -> 34, of which waited for: 8 -> 15; matrix products, arithmetic and copies ran while one was open for 7% -> 4% of each run, Pallas kernels for 0% -> 17%
where the time goes in v2:
time: 227 us
  waiting for transfers between devices  95.4 us (42%)
  starting transfers between devices  52.1 us (23%)
  Pallas kernels  49.2 us (22%)
  between operations  14.8 us (7%)
  local copies, waits for them, and re-layouts  9.04 us (4%)
  other arithmetic  5.99 us (3%)
    ppermute x20, waiting for transfers between devices, shift(): lax.ppermute(x, axis, [(i, (i // 2 + step) % 4 * 2 + i % 2) for i in rang...  40.7 us
    reduce_scatter x1, waiting for transfers between devices, per_device(): separator = lax.psum_scatter(total, 'row', scatter_dimension=0, tiled=True)  38.8 us
    pallas_call x5, Pallas kernels, call(): pl.pallas_call(kernel, out_shape=out, in_specs=[SMEM] * len(scalars) + [V...  38.4 us
    ppermute x20, starting transfers between devices, shift(): lax.ppermute(x, axis, [(i, (i // 2 + step) % 4 * 2 + i % 2) for i in rang...  32.8 us
    ppermute x8, starting transfers between devices, swap(): return lax.ppermute(x, axis, [(i, i ^ 1) for i in range(SIDE)])  16.9 us
    ppermute x8, waiting for transfers between devices, swap(): return lax.ppermute(x, axis, [(i, i ^ 1) for i in range(SIDE)])  14.4 us
    pallas_call x2, Pallas kernels, partial(): pl.pallas_call(functools.partial(partial_kernel, first, count), out_shape...  10.8 us
    unnamed x58, local copies, waits for them, and re-layouts  6.13 us
  transfers between devices with their start and end apart: 34, of which 15 were waited for; matrix products, arithmetic and copies ran while one was open for 4% of the time, Pallas kernels for 17%

profile of v2, /device:TPU:0, one launch (start us, length us, event | category | flops | bytes accessed | tf_op | source)
XLA Modules:
  0.0 226.6 jit_solution(14885693810398621095)
XLA Ops:
  8.7 3.4 %collective-permute-start.4 = (f32[384,384]{1,0:T(8,128)}, f32[384,384]{1,0:T(8,128)S(1)}, u32[]{:S(2)}, u32[]{:S(2)}) collective-permute-start(f32[384,384]{1,0:T(8,128)} %bitcast.29), channel_id=1, source_target_pairs={{0,1},{1,0},{2,3},{3,2},{4,5},{5,4},{6,7},{7,6},{8,9},{9,8},{10,11... | collective-permute-start | bytes 1769480 | tf_op jit(solution)/shard_map/ppermute | solution.py:43
  12.1 3.9 %collective-permute-start.3 = (f32[384,384]{1,0:T(8,128)}, f32[384,384]{1,0:T(8,128)S(1)}, u32[]{:S(2)}, u32[]{:S(2)}) collective-permute-start(f32[384,384]{1,0:T(8,128)} %bitcast.30), channel_id=1, source_target_pairs={{0,4},{1,5},{2,6},{3,7},{4,0},{5,1},{6,2},{7,3},{8,12},{9,13},{10,... | collective-permute-start | bytes 1769480 | tf_op jit(solution)/shard_map/ppermute | solution.py:39
  16.9 2.2 collective-permute-start.2
  20.6 5.1 %collective-permute-done.4.refs_6_.rest_4_ = f32[384,384]{1,0:T(8,128)S(1)} collective-permute-done((f32[384,384]{1,0:T(8,128)}, f32[384,384]{1,0:T(8,128)S(1)}, u32[]{:S(2)}, u32[]{:S(2)}) %collective-permute-start.4) | collective-permute-done | bytes 589856 | tf_op jit(solution)/shard_map/ppermute | solution.py:43
  25.7 2.0 collective-permute-start.5
  27.7 2.5 %collective-permute-start.6 = (f32[384,384]{1,0:T(8,128)S(1)}, f32[384,384]{1,0:T(8,128)}, u32[]{:S(2)}, u32[]{:S(2)}) collective-permute-start(f32[384,384]{1,0:T(8,128)S(1)} %collective-permute-done.4.refs_6_.rest_4_), channel_id=1, source_target_pairs={{0,6},{1,7},{2,0},{3,1},{4,2},{5,3},{6,4},{7,5},{8,14},{9,15},{10,... | collective-permute-start | bytes 1769480 | tf_op jit(solution)/shard_map/ppermute | solution.py:39
  30.4 2.6 %collective-permute-start.7 = (f32[384,384]{1,0:T(8,128)S(1)}, f32[384,384]{1,0:T(8,128)}, u32[]{:S(2)}, u32[]{:S(2)}) collective-permute-start(f32[384,384]{1,0:T(8,128)S(1)} %collective-permute-done.3.refs_5_.rest_3_), channel_id=1, source_target_pairs={{0,1},{1,0},{2,3},{3,2},{4,5},{5,4},{6,7},{7,6},{8,9},{9,8},{10,11... | collective-permute-start | bytes 1769480 | tf_op jit(solution)/shard_map/ppermute | solution.py:43
  37.7 5.0 %collective-permute-done.1.refs_3_.rest_1_ = f32[384,384]{1,0:T(8,128)S(1)} collective-permute-done((f32[384,384]{1,0:T(8,128)}, f32[384,384]{1,0:T(8,128)S(1)}, u32[]{:S(2)}, u32[]{:S(2)}) %collective-permute-start.1) | collective-permute-done | bytes 589856 | tf_op jit(solution)/shard_map/ppermute | solution.py:39
  44.1 10.5 %collective-permute-done.5.refs_7_.rest_5_ = f32[384,384]{1,0:T(8,128)} collective-permute-done((f32[384,384]{1,0:T(8,128)S(1)}, f32[384,384]{1,0:T(8,128)}, u32[]{:S(2)}, u32[]{:S(2)}) %collective-permute-start.5) | collective-permute-done | bytes 589856 | tf_op jit(solution)/shard_map/ppermute | solution.py:39
  56.5 2.2 collective-permute-start.9
  61.1 5.0 %shard_map.78 = (f32[256,256]{1,0:T(8,128)}, f32[256,256]{1,0:T(8,128)}) custom-call(s32[512]{0:T(512)} %pad_add_fusion.place, f32[4096,256]{1,0:T(8,128)} %all-gather.5.cloned.1.call-done.root, f32[256,384]{1,0:T(8,128)} %get-tuple-element.23._.rest_8_.refs_0_), custom_call_target="tpu_custom_call" | custom-call | flops 5000000000 | bytes 15000000 | tf_op jit(solution)/shard_map/pallas_call | solution.py:100
  67.7 11.4 %shard_map.79.refs_5_ = f32[8,384,384]{2,1,0:T(8,128)} custom-call(f32[384,384]{1,0:T(8,128)} %bitcast.34, f32[384,384]{1,0:T(8,128)} %bitcast.35, f32[384,384]{1,0:T(8,128)} %copy-done.7, f32[384,384]{1,0:T(8,128)} %copy-done.8, f32[384,384]{1,0:T(8,128)} %copy-done.6, f32[384,384]{1,0:T(8,128)} %copy-done.5, ...), custom_call_target="tpu_custom_call" | custom-call | flops 12000000000 | bytes 36000000 | tf_op jit(solution)/shard_map/pallas_call | solution.py:100
  84.2 2.9 %collective-permute-start.15 = (f32[256,384]{1,0:T(8,128)}, f32[256,384]{1,0:T(8,128)S(1)}, u32[]{:S(2)}, u32[]{:S(2)}) collective-permute-start(f32[256,384]{1,0:T(8,128)} %get-tuple-element.30.rest_3_), channel_id=1, source_target_pairs={{0,1},{1,0},{2,3},{3,2},{4,5},{5,4},{6,7},{7,6},{8,9},{9,8},{10,11... | collective-permute-start | bytes 1179656 | tf_op jit(solution)/shard_map/ppermute | solution.py:43
  88.9 5.9 %shard_map.81.refs_1_ = f32[256,384]{1,0:T(8,128)} custom-call(s32[5]{0:T(128)} %stack.40.cols, f32[256,384]{1,0:T(8,128)} %get-tuple-element.27.rest_0_, f32[256,384]{1,0:T(8,128)} %get-tuple-element.28.rest_1_, f32[256,384]{1,0:T(8,128)} %get-tuple-element.29.rest_2_, f32[256,384]{1,0:T(8,128)} %get-tuple-element.30.rest_3_, ...), custom_call_target="tpu_custom_call" | custom-call | flops 5000000000 | bytes 15000000 | tf_op jit(solution)/shard_map/pallas_call | solution.py:100
  96.4 5.0 %shard_map.83.refs_0_ = f32[384,256]{1,0:T(8,128)} custom-call(s32[3]{0:T(128)} %pad_add_fusion.1.cols, s32[1]{0:T(128)} %bitcast.1.row, s32[1]{0:T(128)S(6)} %copy.53.live, f32[256,384]{1,0:T(8,128)} %get-tuple-element.32.part, f32[256,384]{1,0:T(8,128)} %copy-done.16, f32[256,384]{1,0:T(8,128)} %copy-done.18, f32[256,384]{1,0:T(8,128)} %copy-done.20, ...), custom_call_target="tpu_custom_call" | custom-call | flops 3000000000 | bytes 9000000 | tf_op jit(solution)/shard_map/pallas_call | solution.py:100
  101.6 2.7 %collective-permute-start.19 = (f32[512,256]{1,0:T(8,128)S(1)}, f32[512,256]{1,0:T(8,128)S(1)}, u32[]{:S(2)}, u32[]{:S(2)}) collective-permute-start(f32[512,256]{1,0:T(8,128)S(1)} %copy-done), channel_id=1, source_target_pairs={{0,1},{1,0},{2,3},{3,2},{4,5},{5,4},{6,7},{7,6},{8,9},{9,8},{10,11... | collective-permute-start | bytes 1572872 | tf_op jit(solution)/shard_map/ppermute | solution.py:43
  105.9 2.5 %collective-permute-start.17 = (f32[512,256]{1,0:T(8,128)S(1)}, f32[512,256]{1,0:T(8,128)S(1)}, u32[]{:S(2)}, u32[]{:S(2)}) collective-permute-start(f32[512,256]{1,0:T(8,128)S(1)} %copy-done), channel_id=1, source_target_pairs={{0,6},{1,7},{2,0},{3,1},{4,2},{5,3},{6,4},{7,5},{8,14},{9,15},{10,... | collective-permute-start | bytes 1572872 | tf_op jit(solution)/shard_map/ppermute | solution.py:39
  108.4 6.8 %collective-permute-done.19.rest_5_.refs_6_ = f32[512,256]{1,0:T(8,128)S(1)} collective-permute-done((f32[512,256]{1,0:T(8,128)S(1)}, f32[512,256]{1,0:T(8,128)S(1)}, u32[]{:S(2)}, u32[]{:S(2)}) %collective-permute-start.19) | collective-permute-done | bytes 524320 | tf_op jit(solution)/shard_map/ppermute | solution.py:43
  115.1 3.2 %collective-permute-start.21 = (f32[512,256]{1,0:T(8,128)S(1)}, f32[512,256]{1,0:T(8,128)}, u32[]{:S(2)}, u32[]{:S(2)}) collective-permute-start(f32[512,256]{1,0:T(8,128)S(1)} %collective-permute-done.19.rest_5_.refs_6_), channel_id=1, source_target_pairs={{0,6},{1,7},{2,0},{3,1},{4,2},{5,3},{6,4},{7,5},{8,14},{9,15},{10,... | collective-permute-start | bytes 1572872 | tf_op jit(solution)/shard_map/ppermute | solution.py:39
  118.4 2.3 %collective-permute-done.18.rest_4_.refs_5_ = f32[512,256]{1,0:T(8,128)S(1)} collective-permute-done((f32[512,256]{1,0:T(8,128)S(1)}, f32[512,256]{1,0:T(8,128)S(1)}, u32[]{:S(2)}, u32[]{:S(2)}) %collective-permute-start.18) | collective-permute-done | bytes 524320 | tf_op jit(solution)/shard_map/ppermute | solution.py:39
  122.8 5.9 %collective-permute-done.16.rest_2_.refs_3_ = f32[512,256]{1,0:T(8,128)S(1)} collective-permute-done((f32[512,256]{1,0:T(8,128)S(1)}, f32[512,256]{1,0:T(8,128)S(1)}, u32[]{:S(2)}, u32[]{:S(2)}) %collective-permute-start.16) | collective-permute-done | bytes 524320 | tf_op jit(solution)/shard_map/ppermute | solution.py:39
  129.9 9.1 %collective-permute-done.20.rest_6_.refs_7_ = f32[512,256]{1,0:T(8,128)S(1)} collective-permute-done((f32[512,256]{1,0:T(8,128)S(1)}, f32[512,256]{1,0:T(8,128)S(1)}, u32[]{:S(2)}, u32[]{:S(2)}) %collective-permute-start.20) | collective-permute-done | bytes 524320 | tf_op jit(solution)/shard_map/ppermute | solution.py:39
  139.8 3.2 %collective-permute-start.24 = (f32[384,256]{1,0:T(8,128)}, f32[384,256]{1,0:T(8,128)S(1)}, u32[]{:S(2)}, u32[]{:S(2)}) collective-permute-start(f32[384,256]{1,0:T(8,128)} %get-tuple-element.35.refs_0_), channel_id=1, source_target_pairs={{0,6},{1,7},{2,0},{3,1},{4,2},{5,3},{6,4},{7,5},{8,14},{9,15},{10,... | collective-permute-start | bytes 1179656 | tf_op jit(solution)/shard_map/ppermute | solution.py:39
  143.1 1.8 collective-permute-start.26
  144.9 11.1 %shard_map.84.refs_5_.coupling = f32[256,384]{1,0:T(8,128)} custom-call(s32[2048]{0:T(1024)} %fusion.8.place, s32[1]{0:T(128)} %bitcast.1.row, s32[1]{0:T(128)S(6)} %copy.53.live, f32[3072,256]{1,0:T(8,128)} %all-gather.7.cloned.1.call-done.rest_0_, f32[512,256]{1,0:T(8,128)} %get-tuple-element.33.rest_1_.refs_2_, f32[512,256]{1,0:T(8,128)} %copy-done.11, ...), custom_call_target="tpu_custom_call" | custom-call | flops 12000000000 | bytes 36000000 | tf_op jit(solution)/shard_map/pallas_call | solution.py:100
  156.0 4.4 %collective-permute-done.23.refs_1_ = f32[384,256]{1,0:T(8,128)S(1)} collective-permute-done((f32[384,256]{1,0:T(8,128)}, f32[384,256]{1,0:T(8,128)S(1)}, u32[]{:S(2)}, u32[]{:S(2)}) %collective-permute-start.23) | collective-permute-done | bytes 393248 | tf_op jit(solution)/shard_map/ppermute | solution.py:39
  162.7 2.6 %collective-permute-start.28 = (f32[384,256]{1,0:T(8,128)}, f32[384,256]{1,0:T(8,128)S(1)}, u32[]{:S(2)}, u32[]{:S(2)}) collective-permute-start(f32[384,256]{1,0:T(8,128)} %get-tuple-element.36.rest_4_), channel_id=1, source_target_pairs={{0,6},{1,7},{2,0},{3,1},{4,2},{5,3},{6,4},{7,5},{8,14},{9,15},{10,... | collective-permute-start | bytes 1179656 | tf_op jit(solution)/shard_map/ppermute | solution.py:39
  165.3 2.2 collective-permute-start.29
  167.5 6.0 %shard_map.87.refs_0_ = f32[3072,384]{1,0:T(8,128)} custom-call(s32[8]{0:T(128)} %stack.41.cols, f32[256,384]{1,0:T(8,128)} %shard_map.84.refs_5_.coupling, f32[384,256]{1,0:T(8,128)} %get-tuple-element.39.rest_0_, f32[384,256]{1,0:T(8,128)} %get-tuple-element.40.rest_1_, f32[384,256]{1,0:T(8,128)} %get-tuple-element.41.rest_2_, ...), custom_call_target="tpu_custom_call" | custom-call | flops 5000000000 | bytes 15000000 | tf_op jit(solution)/shard_map/pallas_call | solution.py:222
  173.6 2.0 collective-permute-done.29.refs_3_.rest_2_
  176.4 4.8 %shard_map.89 = f32[3072,384]{1,0:T(8,128)} custom-call(s32[8]{0:T(128)} %stack.41.cols, f32[256,384]{1,0:T(8,128)} %shard_map.84.refs_5_.coupling, f32[384,256]{1,0:T(8,128)} %copy-done.1, f32[384,256]{1,0:T(8,128)} %copy-done.2, f32[384,256]{1,0:T(8,128)} %copy-done.3, ...), custom_call_target="tpu_custom_call", output_to_operand_aliasing={{}: (6, {})} | custom-call | flops 3000000000 | bytes 9000000 | tf_op jit(solution)/shard_map/pallas_call | solution.py:222
  181.2 38.8 %reduce-scatter.2.cloned.1.call-done = f32[384,384]{1,0:T(8,128)} async-done(((f32[3072,384]{1,0:T(8,128)}), f32[384,384]{1,0:T(8,128)}) %reduce-scatter.2.cloned.1.call-update) | async-done | bytes 589840 | tf_op jit(solution)/shard_map/reduce_scatter | solution.py:294
  (124 shorter events, 32.8 us)
Async XLA Ops:
  7.2 54.0 %all-gather.5.cloned.1.call-start = ((), (), s32[]{:S(2)}) async-start(), calls=%async_computation.1 | async-start | bytes 4718592 | tf_op jit(solution)/shard_map/all_gather | solution.py:246
  7.9 81.0 %all-gather.9.cloned.1.call-start = ((), (), s32[]{:S(2)}) async-start(), calls=%async_computation.4 | async-start | bytes 5308416 | tf_op jit(solution)/shard_map/all_gather | solution.py:248
  8.6 130.4 %all-gather.7.cloned.1.call-start = ((), (), s32[]{:S(2)}) async-start(), calls=%async_computation.2 | async-start | bytes 3538944 | tf_op jit(solution)/shard_map/all_gather | solution.py:277
  8.7 17.0 %collective-permute-start.4 = (f32[384,384]{1,0:T(8,128)}, f32[384,384]{1,0:T(8,128)S(1)}, u32[]{:S(2)}, u32[]{:S(2)}) collective-permute-start(f32[384,384]{1,0:T(8,128)} %bitcast.29), channel_id=1, source_target_pairs={{0,1},{1,0},{2,3},{3,2},{4,5},{5,4},{6,7},{7,6},{8,9},{9,8},{10,11... | collective-permute-start | bytes 1769480 | tf_op jit(solution)/shard_map/ppermute | solution.py:43
  12.1 18.4 %collective-permute-start.3 = (f32[384,384]{1,0:T(8,128)}, f32[384,384]{1,0:T(8,128)S(1)}, u32[]{:S(2)}, u32[]{:S(2)}) collective-permute-start(f32[384,384]{1,0:T(8,128)} %bitcast.30), channel_id=1, source_target_pairs={{0,4},{1,5},{2,6},{3,7},{4,0},{5,1},{6,2},{7,3},{8,12},{9,13},{10,... | collective-permute-start | bytes 1769480 | tf_op jit(solution)/shard_map/ppermute | solution.py:39
  15.9 26.7 %collective-permute-start.1 = (f32[384,384]{1,0:T(8,128)}, f32[384,384]{1,0:T(8,128)S(1)}, u32[]{:S(2)}, u32[]{:S(2)}) collective-permute-start(f32[384,384]{1,0:T(8,128)} %bitcast.31), channel_id=1, source_target_pairs={{0,2},{1,3},{2,4},{3,5},{4,6},{5,7},{6,0},{7,1},{8,10},{9,11},{10,... | collective-permute-start | bytes 1769480 | tf_op jit(solution)/shard_map/ppermute | solution.py:39
  16.9 27.1 %collective-permute-start.2 = (f32[384,384]{1,0:T(8,128)}, f32[384,384]{1,0:T(8,128)S(1)}, u32[]{:S(2)}, u32[]{:S(2)}) collective-permute-start(f32[384,384]{1,0:T(8,128)} %bitcast.32), channel_id=1, source_target_pairs={{0,6},{1,7},{2,0},{3,1},{4,2},{5,3},{6,4},{7,5},{8,14},{9,15},{10,... | collective-permute-start | bytes 1769480 | tf_op jit(solution)/shard_map/ppermute | solution.py:39
  25.7 28.9 %collective-permute-start.5 = (f32[384,384]{1,0:T(8,128)S(1)}, f32[384,384]{1,0:T(8,128)}, u32[]{:S(2)}, u32[]{:S(2)}) collective-permute-start(f32[384,384]{1,0:T(8,128)S(1)} %collective-permute-done.4.refs_6_.rest_4_), channel_id=1, source_target_pairs={{0,2},{1,3},{2,4},{3,5},{4,6},{5,7},{6,0},{7,1},{8,10},{9,11},{10,... | collective-permute-start | bytes 1769480 | tf_op jit(solution)/shard_map/ppermute | solution.py:39
  27.7 27.7 %collective-permute-start.6 = (f32[384,384]{1,0:T(8,128)S(1)}, f32[384,384]{1,0:T(8,128)}, u32[]{:S(2)}, u32[]{:S(2)}) collective-permute-start(f32[384,384]{1,0:T(8,128)S(1)} %collective-permute-done.4.refs_6_.rest_4_), channel_id=1, source_target_pairs={{0,6},{1,7},{2,0},{3,1},{4,2},{5,3},{6,4},{7,5},{8,14},{9,15},{10,... | collective-permute-start | bytes 1769480 | tf_op jit(solution)/shard_map/ppermute | solution.py:39
  30.4 24.9 %collective-permute-start.7 = (f32[384,384]{1,0:T(8,128)S(1)}, f32[384,384]{1,0:T(8,128)}, u32[]{:S(2)}, u32[]{:S(2)}) collective-permute-start(f32[384,384]{1,0:T(8,128)S(1)} %collective-permute-done.3.refs_5_.rest_3_), channel_id=1, source_target_pairs={{0,1},{1,0},{2,3},{3,2},{4,5},{5,4},{6,7},{7,6},{8,9},{9,8},{10,11... | collective-permute-start | bytes 1769480 | tf_op jit(solution)/shard_map/ppermute | solution.py:43
  55.4 23.8 %collective-permute-start.8 = (f32[256,384]{1,0:T(8,128)}, f32[256,384]{1,0:T(8,128)S(1)}, u32[]{:S(2)}, u32[]{:S(2)}) collective-permute-start(f32[256,384]{1,0:T(8,128)} %get-tuple-element.23._.rest_8_.refs_0_), channel_id=1, source_target_pairs={{0,2},{1,3},{2,4},{3,5},{4,6},{5,7},{6,0},{7,1},{8,10},{9,11},{10,... | collective-permute-start | bytes 1179656 | tf_op jit(solution)/shard_map/ppermute | solution.py:39
  56.5 22.7 %collective-permute-start.9 = (f32[256,384]{1,0:T(8,128)}, f32[256,384]{1,0:T(8,128)S(1)}, u32[]{:S(2)}, u32[]{:S(2)}) collective-permute-start(f32[256,384]{1,0:T(8,128)} %get-tuple-element.23._.rest_8_.refs_0_), channel_id=1, source_target_pairs={{0,6},{1,7},{2,0},{3,1},{4,2},{5,3},{6,4},{7,5},{8,14},{9,15},{10,... | collective-permute-start | bytes 1179656 | tf_op jit(solution)/shard_map/ppermute | solution.py:39
  58.7 20.5 %collective-permute-start.10 = (f32[256,384]{1,0:T(8,128)}, f32[256,384]{1,0:T(8,128)S(1)}, u32[]{:S(2)}, u32[]{:S(2)}) collective-permute-start(f32[256,384]{1,0:T(8,128)} %get-tuple-element.23._.rest_8_.refs_0_), channel_id=1, source_target_pairs={{0,4},{1,5},{2,6},{3,7},{4,0},{5,1},{6,2},{7,3},{8,12},{9,13},{10,... | collective-permute-start | bytes 1179656 | tf_op jit(solution)/shard_map/ppermute | solution.py:39
  59.6 19.6 %collective-permute-start.11 = (f32[256,384]{1,0:T(8,128)}, f32[256,384]{1,0:T(8,128)S(1)}, u32[]{:S(2)}, u32[]{:S(2)}) collective-permute-start(f32[256,384]{1,0:T(8,128)} %get-tuple-element.23._.rest_8_.refs_0_), channel_id=1, source_target_pairs={{0,1},{1,0},{2,3},{3,2},{4,5},{5,4},{6,7},{7,6},{8,9},{9,8},{10,11... | collective-permute-start | bytes 1179656 | tf_op jit(solution)/shard_map/ppermute | solution.py:43
  66.1 13.1 %collective-permute-start.12 = (f32[256,256]{1,0:T(8,128)}, f32[256,256]{1,0:T(8,128)S(1)}, u32[]{:S(2)}, u32[]{:S(2)}) collective-permute-start(f32[256,256]{1,0:T(8,128)} %get-tuple-element.25), channel_id=1, source_target_pairs={{0,64},{64,0},{1,65},{65,1},{2,66},{66,2},{3,67},{67,3},{4,68},{68... | collective-permute-start | bytes 786440 | tf_op jit(solution)/shard_map/ppermute | solution.py:47
  81.0 13.8 %collective-permute-start.13 = (f32[256,384]{1,0:T(8,128)}, f32[256,384]{1,0:T(8,128)S(1)}, u32[]{:S(2)}, u32[]{:S(2)}) collective-permute-start(f32[256,384]{1,0:T(8,128)} %get-tuple-element.31.rest_4_), channel_id=1, source_target_pairs={{0,2},{1,3},{2,4},{3,5},{4,6},{5,7},{6,0},{7,1},{8,10},{9,11},{10,... | collective-permute-start | bytes 1179656 | tf_op jit(solution)/shard_map/ppermute | solution.py:39
  82.5 12.3 %collective-permute-start.14 = (f32[256,384]{1,0:T(8,128)}, f32[256,384]{1,0:T(8,128)S(1)}, u32[]{:S(2)}, u32[]{:S(2)}) collective-permute-start(f32[256,384]{1,0:T(8,128)} %get-tuple-element.31.rest_4_), channel_id=1, source_target_pairs={{0,6},{1,7},{2,0},{3,1},{4,2},{5,3},{6,4},{7,5},{8,14},{9,15},{10,... | collective-permute-start | bytes 1179656 | tf_op jit(solution)/shard_map/ppermute | solution.py:39
  84.2 11.2 %collective-permute-start.15 = (f32[256,384]{1,0:T(8,128)}, f32[256,384]{1,0:T(8,128)S(1)}, u32[]{:S(2)}, u32[]{:S(2)}) collective-permute-start(f32[256,384]{1,0:T(8,128)} %get-tuple-element.30.rest_3_), channel_id=1, source_target_pairs={{0,1},{1,0},{2,3},{3,2},{4,5},{5,4},{6,7},{7,6},{8,9},{9,8},{10,11... | collective-permute-start | bytes 1179656 | tf_op jit(solution)/shard_map/ppermute | solution.py:43
  101.5 118.5 %reduce-scatter.2.cloned.1.call-start = ((), (), s32[]{:S(2)}) async-start(), calls=%async_computation.3 | async-start | bytes 5308416 | tf_op jit(solution)/shard_map/reduce_scatter | solution.py:294
  101.6 13.6 %collective-permute-start.19 = (f32[512,256]{1,0:T(8,128)S(1)}, f32[512,256]{1,0:T(8,128)S(1)}, u32[]{:S(2)}, u32[]{:S(2)}) collective-permute-start(f32[512,256]{1,0:T(8,128)S(1)} %copy-done), channel_id=1, source_target_pairs={{0,1},{1,0},{2,3},{3,2},{4,5},{5,4},{6,7},{7,6},{8,9},{9,8},{10,11... | collective-permute-start | bytes 1572872 | tf_op jit(solution)/shard_map/ppermute | solution.py:43
  104.3 16.4 %collective-permute-start.18 = (f32[512,256]{1,0:T(8,128)S(1)}, f32[512,256]{1,0:T(8,128)S(1)}, u32[]{:S(2)}, u32[]{:S(2)}) collective-permute-start(f32[512,256]{1,0:T(8,128)S(1)} %copy-done), channel_id=1, source_target_pairs={{0,4},{1,5},{2,6},{3,7},{4,0},{5,1},{6,2},{7,3},{8,12},{9,13},{10,... | collective-permute-start | bytes 1572872 | tf_op jit(solution)/shard_map/ppermute | solution.py:39
  105.1 23.6 %collective-permute-start.16 = (f32[512,256]{1,0:T(8,128)S(1)}, f32[512,256]{1,0:T(8,128)S(1)}, u32[]{:S(2)}, u32[]{:S(2)}) collective-permute-start(f32[512,256]{1,0:T(8,128)S(1)} %copy-done), channel_id=1, source_target_pairs={{0,2},{1,3},{2,4},{3,5},{4,6},{5,7},{6,0},{7,1},{8,10},{9,11},{10,... | collective-permute-start | bytes 1572872 | tf_op jit(solution)/shard_map/ppermute | solution.py:39
  105.9 24.1 %collective-permute-start.17 = (f32[512,256]{1,0:T(8,128)S(1)}, f32[512,256]{1,0:T(8,128)S(1)}, u32[]{:S(2)}, u32[]{:S(2)}) collective-permute-start(f32[512,256]{1,0:T(8,128)S(1)} %copy-done), channel_id=1, source_target_pairs={{0,6},{1,7},{2,0},{3,1},{4,2},{5,3},{6,4},{7,5},{8,14},{9,15},{10,... | collective-permute-start | bytes 1572872 | tf_op jit(solution)/shard_map/ppermute | solution.py:39
  115.1 23.9 %collective-permute-start.20 = (f32[512,256]{1,0:T(8,128)S(1)}, f32[512,256]{1,0:T(8,128)S(1)}, u32[]{:S(2)}, u32[]{:S(2)}) collective-permute-start(f32[512,256]{1,0:T(8,128)S(1)} %collective-permute-done.19.rest_5_.refs_6_), channel_id=1, source_target_pairs={{0,2},{1,3},{2,4},{3,5},{4,6},{5,7},{6,0},{7,1},{8,10},{9,11},{10,... | collective-permute-start | bytes 1572872 | tf_op jit(solution)/shard_map/ppermute | solution.py:39
  115.1 23.9 %collective-permute-start.21 = (f32[512,256]{1,0:T(8,128)S(1)}, f32[512,256]{1,0:T(8,128)}, u32[]{:S(2)}, u32[]{:S(2)}) collective-permute-start(f32[512,256]{1,0:T(8,128)S(1)} %collective-permute-done.19.rest_5_.refs_6_), channel_id=1, source_target_pairs={{0,6},{1,7},{2,0},{3,1},{4,2},{5,3},{6,4},{7,5},{8,14},{9,15},{10,... | collective-permute-start | bytes 1572872 | tf_op jit(solution)/shard_map/ppermute | solution.py:39
  120.6 18.4 %collective-permute-start.22 = (f32[512,256]{1,0:T(8,128)S(1)}, f32[512,256]{1,0:T(8,128)}, u32[]{:S(2)}, u32[]{:S(2)}) collective-permute-start(f32[512,256]{1,0:T(8,128)S(1)} %collective-permute-done.18.rest_4_.refs_5_), channel_id=1, source_target_pairs={{0,1},{1,0},{2,3},{3,2},{4,5},{5,4},{6,7},{7,6},{8,9},{9,8},{10,11... | collective-permute-start | bytes 1572872 | tf_op jit(solution)/shard_map/ppermute | solution.py:43
  139.8 20.5 %collective-permute-start.23 = (f32[384,256]{1,0:T(8,128)}, f32[384,256]{1,0:T(8,128)S(1)}, u32[]{:S(2)}, u32[]{:S(2)}) collective-permute-start(f32[384,256]{1,0:T(8,128)} %get-tuple-element.35.refs_0_), channel_id=1, source_target_pairs={{0,2},{1,3},{2,4},{3,5},{4,6},{5,7},{6,0},{7,1},{8,10},{9,11},{10,... | collective-permute-start | bytes 1179656 | tf_op jit(solution)/shard_map/ppermute | solution.py:39
  139.8 20.5 %collective-permute-start.24 = (f32[384,256]{1,0:T(8,128)}, f32[384,256]{1,0:T(8,128)S(1)}, u32[]{:S(2)}, u32[]{:S(2)}) collective-permute-start(f32[384,256]{1,0:T(8,128)} %get-tuple-element.35.refs_0_), channel_id=1, source_target_pairs={{0,6},{1,7},{2,0},{3,1},{4,2},{5,3},{6,4},{7,5},{8,14},{9,15},{10,... | collective-permute-start | bytes 1179656 | tf_op jit(solution)/shard_map/ppermute | solution.py:39
  143.1 17.3 %collective-permute-start.25 = (f32[384,256]{1,0:T(8,128)}, f32[384,256]{1,0:T(8,128)S(1)}, u32[]{:S(2)}, u32[]{:S(2)}) collective-permute-start(f32[384,256]{1,0:T(8,128)} %get-tuple-element.35.refs_0_), channel_id=1, source_target_pairs={{0,4},{1,5},{2,6},{3,7},{4,0},{5,1},{6,2},{7,3},{8,12},{9,13},{10,... | collective-permute-start | bytes 1179656 | tf_op jit(solution)/shard_map/ppermute | solution.py:39
  143.1 17.3 %collective-permute-start.26 = (f32[384,256]{1,0:T(8,128)}, f32[384,256]{1,0:T(8,128)S(1)}, u32[]{:S(2)}, u32[]{:S(2)}) collective-permute-start(f32[384,256]{1,0:T(8,128)} %get-tuple-element.35.refs_0_), channel_id=1, source_target_pairs={{0,1},{1,0},{2,3},{3,2},{4,5},{5,4},{6,7},{7,6},{8,9},{9,8},{10,11... | collective-permute-start | bytes 1179656 | tf_op jit(solution)/shard_map/ppermute | solution.py:43
  162.1 11.5 %collective-permute-start.27 = (f32[384,256]{1,0:T(8,128)}, f32[384,256]{1,0:T(8,128)S(1)}, u32[]{:S(2)}, u32[]{:S(2)}) collective-permute-start(f32[384,256]{1,0:T(8,128)} %get-tuple-element.36.rest_4_), channel_id=1, source_target_pairs={{0,2},{1,3},{2,4},{3,5},{4,6},{5,7},{6,0},{7,1},{8,10},{9,11},{10,... | collective-permute-start | bytes 1179656 | tf_op jit(solution)/shard_map/ppermute | solution.py:39
  162.7 10.9 %collective-permute-start.28 = (f32[384,256]{1,0:T(8,128)}, f32[384,256]{1,0:T(8,128)S(1)}, u32[]{:S(2)}, u32[]{:S(2)}) collective-permute-start(f32[384,256]{1,0:T(8,128)} %get-tuple-element.36.rest_4_), channel_id=1, source_target_pairs={{0,6},{1,7},{2,0},{3,1},{4,2},{5,3},{6,4},{7,5},{8,14},{9,15},{10,... | collective-permute-start | bytes 1179656 | tf_op jit(solution)/shard_map/ppermute | solution.py:39
  (30 other events, 241.7 us)
Sparse Core Ops, SparseCore 0:
  9.7 34.5 all-gather.4
  46.0 34.2 all-gather.8
  101.6 26.4 all-gather.6
  181.3 38.6 reduce-scatter.1

commit v3 on v2

--- a/solution.py
+++ b/solution.py
@@ -21,7 +21,6 @@
 VMEM = pl.BlockSpec(memory_space=pltpu.VMEM)
 SMEM = pl.BlockSpec(memory_space=pltpu.SMEM)
 ANY = pl.BlockSpec(memory_space=pl.ANY)
-
 
 def hold(arrays, deps):
     n = len(arrays)
@@ -34,35 +33,28 @@
         compiler_params=pltpu.CompilerParams(vmem_limit_bytes=60 * 2**20),
     )(*arrays, *deps)
 
-
 def shift(x, axis, step):
     return lax.ppermute(x, axis, [(i, (i // 2 + step) % 4 * 2 + i % 2) for i in range(SIDE)])
 
-
 def swap(x, axis):
     return lax.ppermute(x, axis, [(i, i ^ 1) for i in range(SIDE)])
 
-
 def swap_group(x):
     return lax.ppermute(x, "grp", [(0, 1), (1, 0)])
 
-
 ORDER = ((0, 0), (-1, 0), (1, 0), (2, 0), (0, 1), (-1, 1), (1, 1), (2, 1))
-
 
 def near_col(x):
     return [x, shift(x, "col", 1), shift(x, "col", -1), shift(x, "col", 2), swap(x, "col")]
 
-
 def rest_col(far, other):
     return [shift(other, "col", 1), shift(other, "col", -1), swap(far, "col")]
 
-
-def gather_col(x, meanwhile=()):
-    *near, far, other = near_col(x)
-    far, other, *rest = hold([far, other, *meanwhile], near[1:])
-    return [*near, far, other, *rest_col(far, other)], rest
-
+def gather_col(x):
+    n = x.shape[0] // 2
+    before, next_, other = shift(x, "col", 1), shift(x, "col", -1), swap(x, "col")
+    far = jnp.concatenate([shift(before[:n], "col", 1), shift(next_[n:], "col", -1)], axis=0)
+    return [x, before, next_, far, other, *rest_col(far, other)]
 
 def fetch(refs, buffer, sems):
     copies = [pltpu.make_async_copy(ref, buffer.at[p], sems.at[p]) for p, ref in enumerate(refs)]
@@ -70,11 +62,9 @@
         copy.start()
     return copies
 
-
 def ids_of(axis):
     i = lax.axis_index(axis)
     return jnp.stack([(i // 2 + ring) % 4 * 2 + jnp.bitwise_xor(i % 2, pair) for ring, pair in ORDER]).astype(jnp.int32)
-
 
 def place_of(block, axis):
     i = lax.axis_index(axis)
@@ -82,19 +72,14 @@
     first = jnp.where(ring == 3, 1, jnp.where(ring == 0, 0, ring + 1))
     return first + 4 * jnp.bitwise_xor(block % 2, i % 2)
 
-
 def split(x):
     high = x.astype(bf16)
     return high, (x - high.astype(f32)).astype(bf16)
 
-
-def dot(a, b):
-    return jnp.dot(a, b, preferred_element_type=f32)
-
-
 def dot3(a, b):
-    return dot(a[0], b[0]) + (dot(a[0], b[1]) + dot(a[1], b[0]))
-
+    left = jnp.concatenate([a[0], a[0], a[1]], axis=1)
+    right = jnp.concatenate([b[0], b[1], b[0]], axis=0)
+    return jnp.dot(left, right, preferred_element_type=f32)
 
 def call(kernel, out, scalars, blocks, arrays, scratch, copies, work):
     return pl.pallas_call(
@@ -107,10 +92,8 @@
         cost_estimate=pl.CostEstimate(flops=work * 10**9, bytes_accessed=work * 3 * 10**6, transcendentals=0),
     )(*scalars, *blocks, *arrays)
 
-
 def array(*shape, dtype=f32):
     return jax.ShapeDtypeStruct(shape, dtype)
-
 
 def update_sum(cols, below, diag, below_buf, diag_buf, sems):
     n = len(below)
@@ -130,18 +113,15 @@
         total += dot3(split(below_buf[p]), split(diag_buf[p]))
     return total
 
-
 def update_near_kernel(cols, *rest):
     out, *scratch = rest[6:]
     out[...] = update_sum(cols, rest[:5], rest[5], *scratch)
-
 
 def update_kernel(cols, row, live, part, *rest):
     flipped, *scratch = rest[4:]
     total = part[...] + update_sum(cols, rest[:3], rest[3], *scratch)
     ids = row[0] * BAND + lax.broadcasted_iota(jnp.int32, (BAND, WIDE), 0)
     flipped[...] = jnp.where(ids < live[0], total, 0.0).T
-
 
 def pick_rows(place, source, out, first, count):
     step = 32
@@ -154,7 +134,6 @@
         return carry
 
     lax.fori_loop(0, count // step, body, 0)
-
 
 def root_rows_kernel(place, root, _, own, other, source, found, sems):
     copy = pltpu.make_async_copy(root, source, sems.at[0])
@@ -163,7 +142,6 @@
     for half, out in enumerate((own, other)):
         pick_rows(place, source, found, half * BAND, BAND)
         out[...] = found[...].T
-
 
 def coupling_kernel(place, row, live, *rest):
     update, pieces, out, update_buf, source, found, sems = rest[0], rest[1:9], *rest[9:]
@@ -185,7 +163,6 @@
     ids = row[0] * BAND + lax.broadcasted_iota(jnp.int32, (BAND, WIDE), 0)
     out[...] = jnp.where(ids < live[0], -total.T, 0.0)
 
-
 def gram_kernel(diag, *rest):
     pieces, out, buffer, sems = rest[:8], *rest[9:]
     copies = fetch(pieces, buffer, sems)
@@ -193,7 +170,6 @@
     for p in range(8):
         copies[p].wait()
         out[p] = dot3(split(buffer[p].T), right)
-
 
 def partial_kernel(first, count, cols, coupling, *rest):
     update, gram, out, update_buf, gram_buf, out_buf, sems = rest[:count], rest[count], *rest[-5:]
@@ -214,7 +190,6 @@
         sent[-1].start()
     for copy in sent:
         copy.wait()
-
 
 def partial(first, update, cols, coupling, gram, onto=None):
     count = len(update)
@@ -235,7 +210,6 @@
         cost_estimate=pl.CostEstimate(flops=count * 10**9, bytes_accessed=count * 3 * 10**6, transcendentals=0),
     )(*given)
 
-
 def per_device(root_inverse, ancestor_map, live_rows, factor_below, diag_inverse, tile_mask):
     row, group = lax.axis_index("row"), lax.axis_index("grp")
     cols = ids_of("col")
@@ -247,8 +221,7 @@
 
     diag_cols = lax.all_gather(diag_block, "row", axis=0, tiled=True)
 
-    diag_all = near_col(diag_block)
-    diag_all += rest_col(*diag_all[3:])
+    diag_all = gather_col(diag_block)
     tile_keep = jnp.repeat(jnp.repeat(tile_mask[0], TILE, axis=0), TILE, axis=1).astype(f32)
     below, other_map = hold([factor_below[0] * tile_keep, other_map[None]], diag_all)
 
@@ -275,8 +248,7 @@
         [((3, BAND, WIDE), f32), ((3, WIDE, WIDE), f32)], 6, 3,
     )
     update_rows = lax.all_gather(flipped, "row", axis=0, tiled=True)
-    picked_all = near_col(picked)
-    picked_all += rest_col(*picked_all[3:])
+    picked_all = gather_col(picked)
     flipped, gram = hold([flipped, gram], picked_all)
 
     half = (own_map // (ROOT // 2) != group).astype(jnp.int32)
@@ -286,14 +258,13 @@
         [((SIDE, WIDE, BAND), f32), ((ROOT, BAND), f32), ((BAND, BAND), f32)], 16, 12,
     )
     update_near = near_col(flipped)
-    update_near = hold(update_near, [coupling])
+
     update_rest = rest_col(*update_near[3:])
     total = partial(0, update_near, cols, coupling, gram)
     (total,) = hold([total], update_rest)
     total = partial(5, update_rest, cols, coupling, gram, total)
     separator = lax.psum_scatter(total, "row", scatter_dimension=0, tiled=True)
     return (coupling[None], separator[None])
-
 
 def solution(mesh):
     return jax.shard_map(

time: 227 us -> 217 us (0.956)
  waiting for transfers between devices: 95.4 us -> 82.6 us
  starting transfers between devices: 52.1 us -> 56.7 us
    ppermute x20 -> x22, waiting for transfers between devices: 40.7 us -> 28.8 us  [shift(): lax.ppermute(x, axis, [(i, (i // 2 + step) % 4 * 2 + i % 2) for i in rang...]
    ppermute x8, waiting for transfers between devices: 14.4 us -> 9.97 us  [swap(): return lax.ppermute(x, axis, [(i, i ^ 1) for i in range(SIDE)])]
    ppermute x20 -> x22, starting transfers between devices: 32.8 us -> 37.3 us  [shift(): lax.ppermute(x, axis, [(i, (i // 2 + step) % 4 * 2 + i % 2) for i in rang...]
    reduce_scatter x1, waiting for transfers between devices: 38.8 us -> 42.4 us  [per_device(): separator = lax.psum_scatter(total, 'row', scatter_dimension=0, tiled=True)]
    unnamed x58 -> x66, local copies, waits for them, and re-layouts: 6.13 us -> 5.43 us
  transfers between devices with their start and end apart: 34 -> 36, of which waited for: 15 -> 13; matrix products, arithmetic and copies ran while one was open for 4% -> 5% of each run, Pallas kernels for 17% -> 17%
where the time goes in v3:
time: 217 us
  waiting for transfers between devices  82.6 us (38%)
  starting transfers between devices  56.7 us (26%)
  Pallas kernels  47.4 us (22%)
  between operations  14.9 us (7%)
  local copies, waits for them, and re-layouts  10.2 us (5%)
  other arithmetic  5.14 us (2%)
    reduce_scatter x1, waiting for transfers between devices, per_device(): separator = lax.psum_scatter(total, 'row', scatter_dimension=0, tiled=True)  42.4 us
    ppermute x22, starting transfers between devices, shift(): lax.ppermute(x, axis, [(i, (i // 2 + step) % 4 * 2 + i % 2) for i in rang...  37.3 us
    pallas_call x5, Pallas kernels, call(): pl.pallas_call(kernel, out_shape=out, in_specs=[SMEM] * len(scalars) + [V...  36.6 us
    ppermute x22, waiting for transfers between devices, shift(): lax.ppermute(x, axis, [(i, (i // 2 + step) % 4 * 2 + i % 2) for i in rang...  28.8 us
    ppermute x8, starting transfers between devices, swap(): return lax.ppermute(x, axis, [(i, i ^ 1) for i in range(SIDE)])  17.4 us
    pallas_call x2, Pallas kernels, partial(): pl.pallas_call(functools.partial(partial_kernel, first, count), out_shape...  10.8 us
    ppermute x8, waiting for transfers between devices, swap(): return lax.ppermute(x, axis, [(i, i ^ 1) for i in range(SIDE)])  9.97 us
    unnamed x66, local copies, waits for them, and re-layouts  5.43 us
  transfers between devices with their start and end apart: 36, of which 13 were waited for; matrix products, arithmetic and copies ran while one was open for 5% of the time, Pallas kernels for 17%

profile of v3, /device:TPU:0, one launch (start us, length us, event | category | flops | bytes accessed | tf_op | source)
XLA Modules:
  0.0 216.9 jit_solution(18093867476202706071)
XLA Ops:
  8.7 2.1 collective-permute-start.1
  10.8 2.2 %collective-permute-start.2 = (f32[384,384]{1,0:T(8,128)}, f32[384,384]{1,0:T(8,128)S(1)}, u32[]{:S(2)}, u32[]{:S(2)}) collective-permute-start(f32[384,384]{1,0:T(8,128)} %bitcast.30), channel_id=1, source_target_pairs={{0,6},{1,7},{2,0},{3,1},{4,2},{5,3},{6,4},{7,5},{8,14},{9,15},{10,... | collective-permute-start | bytes 1769480 | tf_op jit(solution)/shard_map/ppermute | solution.py:37
  13.0 3.2 %collective-permute-start.5 = (f32[384,384]{1,0:T(8,128)}, f32[384,384]{1,0:T(8,128)S(1)}, u32[]{:S(2)}, u32[]{:S(2)}) collective-permute-start(f32[384,384]{1,0:T(8,128)} %bitcast.31), channel_id=1, source_target_pairs={{0,1},{1,0},{2,3},{3,2},{4,5},{5,4},{6,7},{7,6},{8,9},{9,8},{10,11... | collective-permute-start | bytes 1769480 | tf_op jit(solution)/shard_map/ppermute | solution.py:40
  16.2 10.3 %collective-permute-done.1.refs_3_.rest_1_ = f32[384,384]{1,0:T(8,128)S(1)} collective-permute-done((f32[384,384]{1,0:T(8,128)}, f32[384,384]{1,0:T(8,128)S(1)}, u32[]{:S(2)}, u32[]{:S(2)}) %collective-permute-start.1) | collective-permute-done | bytes 589856 | tf_op jit(solution)/shard_map/ppermute | solution.py:37
  29.0 3.1 %collective-permute-start.4 = (f32[192,384]{1,0:T(8,128)}, f32[192,384]{1,0:T(8,128)}, u32[]{:S(2)}, u32[]{:S(2)}) collective-permute-start(f32[192,384]{1,0:T(8,128)} %slice.21), channel_id=1, source_target_pairs={{0,6},{1,7},{2,0},{3,1},{4,2},{5,3},{6,4},{7,5},{8,14},{9,15},{10,... | collective-permute-start | bytes 884744 | tf_op jit(solution)/shard_map/ppermute | solution.py:37
  33.0 3.2 %collective-permute-start.7 = (f32[384,384]{1,0:T(8,128)S(1)}, f32[384,384]{1,0:T(8,128)}, u32[]{:S(2)}, u32[]{:S(2)}) collective-permute-start(f32[384,384]{1,0:T(8,128)S(1)} %collective-permute-done.5.refs_6_.rest_4_), channel_id=1, source_target_pairs={{0,6},{1,7},{2,0},{3,1},{4,2},{5,3},{6,4},{7,5},{8,14},{9,15},{10,... | collective-permute-start | bytes 1769480 | tf_op jit(solution)/shard_map/ppermute | solution.py:37
  36.6 3.3 %collective-permute-done.4 = f32[192,384]{1,0:T(8,128)} collective-permute-done((f32[192,384]{1,0:T(8,128)}, f32[192,384]{1,0:T(8,128)}, u32[]{:S(2)}, u32[]{:S(2)}) %collective-permute-start.4) | collective-permute-done | bytes 294944 | tf_op jit(solution)/shard_map/ppermute | solution.py:37
  40.9 3.0 %collective-permute-start.8 = (f32[384,384]{1,0:T(8,128)S(1)}, f32[384,384]{1,0:T(8,128)}, u32[]{:S(2)}, u32[]{:S(2)}) collective-permute-start(f32[384,384]{1,0:T(8,128)S(1)} %constant_dynamic-update-slice_fusion.refs_5_.rest_3_), channel_id=1, source_target_pairs={{0,1},{1,0},{2,3},{3,2},{4,5},{5,4},{6,7},{7,6},{8,9},{9,8},{10,11... | collective-permute-start | bytes 1769480 | tf_op jit(solution)/shard_map/ppermute | solution.py:40
  50.1 3.2 %collective-permute-done.8.refs_9_.rest_7_ = f32[384,384]{1,0:T(8,128)} collective-permute-done((f32[384,384]{1,0:T(8,128)S(1)}, f32[384,384]{1,0:T(8,128)}, u32[]{:S(2)}, u32[]{:S(2)}) %collective-permute-start.8) | collective-permute-done | bytes 589856 | tf_op jit(solution)/shard_map/ppermute | solution.py:40
  53.6 3.6 %collective-permute-start.10 = (f32[256,384]{1,0:T(8,128)}, f32[256,384]{1,0:T(8,128)S(1)}, u32[]{:S(2)}, u32[]{:S(2)}) collective-permute-start(f32[256,384]{1,0:T(8,128)} %get-tuple-element.18._.rest_8_.refs_0_), channel_id=1, source_target_pairs={{0,6},{1,7},{2,0},{3,1},{4,2},{5,3},{6,4},{7,5},{8,14},{9,15},{10,... | collective-permute-start | bytes 1179656 | tf_op jit(solution)/shard_map/ppermute | solution.py:37
  58.6 2.9 %collective-permute-start.12 = (f32[256,384]{1,0:T(8,128)}, f32[256,384]{1,0:T(8,128)S(1)}, u32[]{:S(2)}, u32[]{:S(2)}) collective-permute-start(f32[256,384]{1,0:T(8,128)} %get-tuple-element.18._.rest_8_.refs_0_), channel_id=1, source_target_pairs={{0,1},{1,0},{2,3},{3,2},{4,5},{5,4},{6,7},{7,6},{8,9},{9,8},{10,11... | collective-permute-start | bytes 1179656 | tf_op jit(solution)/shard_map/ppermute | solution.py:40
  62.8 5.0 %shard_map.78 = (f32[256,256]{1,0:T(8,128)}, f32[256,256]{1,0:T(8,128)}) custom-call(s32[512]{0:T(512)} %pad_add_fusion.place, f32[4096,256]{1,0:T(8,128)} %all-gather.5.cloned.1.call-done.root, f32[256,384]{1,0:T(8,128)} %get-tuple-element.18._.rest_8_.refs_0_), custom_call_target="tpu_custom_call" | custom-call | flops 5000000000 | bytes 15000000 | tf_op jit(solution)/shard_map/pallas_call | solution.py:85
  67.9 10.1 %shard_map.79.refs_5_ = f32[8,384,384]{2,1,0:T(8,128)} custom-call(f32[384,384]{1,0:T(8,128)} %bitcast.33, f32[384,384]{1,0:T(8,128)} %bitcast.34, f32[384,384]{1,0:T(8,128)} %copy-done.4, f32[384,384]{1,0:T(8,128)} %copy-done.5, f32[384,384]{1,0:T(8,128)} %copy-done.6, f32[384,384]{1,0:T(8,128)} %copy-done.11, ...), custom_call_target="tpu_custom_call" | custom-call | flops 12000000000 | bytes 36000000 | tf_op jit(solution)/shard_map/pallas_call | solution.py:85
  81.3 1.8 collective-permute-start.15
  84.8 1.8 pad_maximum_fusion.refs_0_
  86.6 5.5 %shard_map.81.refs_1_ = f32[256,384]{1,0:T(8,128)} custom-call(s32[5]{0:T(128)} %stack.40.cols, f32[256,384]{1,0:T(8,128)} %get-tuple-element.22.rest_0_, f32[256,384]{1,0:T(8,128)} %get-tuple-element.23.rest_1_, f32[256,384]{1,0:T(8,128)} %get-tuple-element.24.rest_2_, f32[256,384]{1,0:T(8,128)} %get-tuple-element.25.rest_3_, ...), custom_call_target="tpu_custom_call" | custom-call | flops 5000000000 | bytes 15000000 | tf_op jit(solution)/shard_map/pallas_call | solution.py:85
  93.8 4.8 %shard_map.83.refs_0_ = f32[384,256]{1,0:T(8,128)} custom-call(s32[3]{0:T(128)} %pad_add_fusion.1.cols, s32[1]{0:T(128)} %bitcast.1.row, s32[1]{0:T(128)S(6)} %copy.45.live, f32[256,384]{1,0:T(8,128)} %get-tuple-element.27.part, f32[256,384]{1,0:T(8,128)} %copy-done.15, f32[256,384]{1,0:T(8,128)} %copy-done.16, f32[256,384]{1,0:T(8,128)} %copy-done.17, ...), custom_call_target="tpu_custom_call" | custom-call | flops 3000000000 | bytes 9000000 | tf_op jit(solution)/shard_map/pallas_call | solution.py:85
  98.9 3.1 %collective-permute-start.18 = (f32[512,256]{1,0:T(8,128)S(1)}, f32[512,256]{1,0:T(8,128)S(1)}, u32[]{:S(2)}, u32[]{:S(2)}) collective-permute-start(f32[512,256]{1,0:T(8,128)S(1)} %copy-done), channel_id=1, source_target_pairs={{0,6},{1,7},{2,0},{3,1},{4,2},{5,3},{6,4},{7,5},{8,14},{9,15},{10,... | collective-permute-start | bytes 1572872 | tf_op jit(solution)/shard_map/ppermute | solution.py:37
  102.0 1.9 collective-permute-start.21
  103.9 8.0 %collective-permute-done.17.rest_2_.refs_3_ = f32[512,256]{1,0:T(8,128)S(1)} collective-permute-done((f32[512,256]{1,0:T(8,128)S(1)}, f32[512,256]{1,0:T(8,128)S(1)}, u32[]{:S(2)}, u32[]{:S(2)}) %collective-permute-start.17) | collective-permute-done | bytes 524320 | tf_op jit(solution)/shard_map/ppermute | solution.py:37
  112.1 3.3 %collective-permute-start.20 = (f32[256,256]{1,0:T(8,128)S(1)}, f32[256,256]{1,0:T(8,128)S(1)}, u32[]{:S(2)}, u32[]{:S(2)}) collective-permute-start(f32[256,256]{1,0:T(8,128)S(1)} %slice.23), channel_id=1, source_target_pairs={{0,6},{1,7},{2,0},{3,1},{4,2},{5,3},{6,4},{7,5},{8,14},{9,15},{10,... | collective-permute-start | bytes 786440 | tf_op jit(solution)/shard_map/ppermute | solution.py:37
  115.4 3.2 %collective-permute-start.23 = (f32[512,256]{1,0:T(8,128)S(1)}, f32[512,256]{1,0:T(8,128)S(1)}, u32[]{:S(2)}, u32[]{:S(2)}) collective-permute-start(f32[512,256]{1,0:T(8,128)S(1)} %collective-permute-done.21.rest_5_.refs_6_), channel_id=1, source_target_pairs={{0,6},{1,7},{2,0},{3,1},{4,2},{5,3},{6,4},{7,5},{8,14},{9,15},{10,... | collective-permute-start | bytes 1572872 | tf_op jit(solution)/shard_map/ppermute | solution.py:37
  120.4 1.7 collective-permute-start.24
  123.5 2.5 %collective-permute-done.22.rest_6_.refs_7_ = f32[512,256]{1,0:T(8,128)S(1)} collective-permute-done((f32[512,256]{1,0:T(8,128)S(1)}, f32[512,256]{1,0:T(8,128)S(1)}, u32[]{:S(2)}, u32[]{:S(2)}) %collective-permute-start.22) | collective-permute-done | bytes 524320 | tf_op jit(solution)/shard_map/ppermute | solution.py:37
  126.0 6.1 %collective-permute-done.24.rest_8_.refs_9_ = f32[512,256]{1,0:T(8,128)} collective-permute-done((f32[512,256]{1,0:T(8,128)S(1)}, f32[512,256]{1,0:T(8,128)}, u32[]{:S(2)}, u32[]{:S(2)}) %collective-permute-start.24) | collective-permute-done | bytes 524320 | tf_op jit(solution)/shard_map/ppermute | solution.py:40
  134.7 2.6 %collective-permute-start.30 = (f32[384,256]{1,0:T(8,128)}, f32[384,256]{1,0:T(8,128)S(1)}, u32[]{:S(2)}, u32[]{:S(2)}) collective-permute-start(f32[384,256]{1,0:T(8,128)} %get-tuple-element.30.rest_0_), channel_id=1, source_target_pairs={{0,2},{1,3},{2,4},{3,5},{4,6},{5,7},{6,0},{7,1},{8,10},{9,11},{10,... | collective-permute-start | bytes 1179656 | tf_op jit(solution)/shard_map/ppermute | solution.py:37
  137.9 11.1 %shard_map.84.coupling = f32[256,384]{1,0:T(8,128)} custom-call(s32[2048]{0:T(1024)} %fusion.8.place, s32[1]{0:T(128)} %bitcast.1.row, s32[1]{0:T(128)S(6)} %copy.45.live, f32[3072,256]{1,0:T(8,128)} %all-gather.7.cloned.1.call-done.rest_0_, f32[512,256]{1,0:T(8,128)} %get-tuple-element.28.rest_1_.refs_2_, f32[512,256]{1,0:T(8,128)} %copy-done.7, ...), custom_call_target="tpu_custom_call" | custom-call | flops 12000000000 | bytes 36000000 | tf_op jit(solution)/shard_map/pallas_call | solution.py:85
  150.6 1.8 collective-permute-start.27
  152.4 2.1 collective-permute-start.29
  155.4 6.0 %shard_map.86.refs_0_ = f32[3072,384]{1,0:T(8,128)} custom-call(s32[8]{0:T(128)} %stack.41.cols, f32[256,384]{1,0:T(8,128)} %shard_map.84.coupling, f32[384,256]{1,0:T(8,128)} %get-tuple-element.30.rest_0_, f32[384,256]{1,0:T(8,128)} %copy-done.29, f32[384,256]{1,0:T(8,128)} %copy-done.30, f32[384,256]{1,0:T(8,128)} %copy-done.28, f32[384,256]{1,0:T(8,128)} %copy-done.27, ...), custom_call_target="tpu_custom_call" | custom-call | flops 5000000000 | bytes 15000000 | tf_op jit(solution)/shard_map/pallas_call | solution.py:197
  163.2 4.8 %shard_map.88 = f32[3072,384]{1,0:T(8,128)} custom-call(s32[8]{0:T(128)} %stack.41.cols, f32[256,384]{1,0:T(8,128)} %shard_map.84.coupling, f32[384,256]{1,0:T(8,128)} %copy-done.1, f32[384,256]{1,0:T(8,128)} %copy-done.2, f32[384,256]{1,0:T(8,128)} %copy-done.3, f32[8,384,384]{2,1,0:T(8,128)} %get-tuple-element.31.rest_5_.rest_3_, ...), custom_call_target="tpu_custom_call", output_to_operand_aliasing={{}: (6, {})} | custom-call | flops 3000000000 | bytes 9000000 | tf_op jit(solution)/shard_map/pallas_call | solution.py:197
  168.0 42.4 %reduce-scatter.2.cloned.1.call-done = f32[384,384]{1,0:T(8,128)} async-done(((f32[3072,384]{1,0:T(8,128)}), f32[384,384]{1,0:T(8,128)}) %reduce-scatter.2.cloned.1.call-update) | async-done | bytes 589840 | tf_op jit(solution)/shard_map/reduce_scatter | solution.py:266
  (141 shorter events, 32.1 us)
Async XLA Ops:
  7.2 55.6 %all-gather.5.cloned.1.call-start = ((), (), s32[]{:S(2)}) async-start(), calls=%async_computation.1 | async-start | bytes 4718592 | tf_op jit(solution)/shard_map/all_gather | solution.py:220
  7.9 78.6 %all-gather.9.cloned.1.call-start = ((), (), s32[]{:S(2)}) async-start(), calls=%async_computation.4 | async-start | bytes 5308416 | tf_op jit(solution)/shard_map/all_gather | solution.py:222
  8.7 123.4 %all-gather.7.cloned.1.call-start = ((), (), s32[]{:S(2)}) async-start(), calls=%async_computation.2 | async-start | bytes 3538944 | tf_op jit(solution)/shard_map/all_gather | solution.py:250
  8.7 17.7 %collective-permute-start.1 = (f32[384,384]{1,0:T(8,128)}, f32[384,384]{1,0:T(8,128)S(1)}, u32[]{:S(2)}, u32[]{:S(2)}) collective-permute-start(f32[384,384]{1,0:T(8,128)} %bitcast.29), channel_id=1, source_target_pairs={{0,2},{1,3},{2,4},{3,5},{4,6},{5,7},{6,0},{7,1},{8,10},{9,11},{10,... | collective-permute-start | bytes 1769480 | tf_op jit(solution)/shard_map/ppermute | solution.py:37
  10.8 17.4 %collective-permute-start.2 = (f32[384,384]{1,0:T(8,128)}, f32[384,384]{1,0:T(8,128)S(1)}, u32[]{:S(2)}, u32[]{:S(2)}) collective-permute-start(f32[384,384]{1,0:T(8,128)} %bitcast.30), channel_id=1, source_target_pairs={{0,6},{1,7},{2,0},{3,1},{4,2},{5,3},{6,4},{7,5},{8,14},{9,15},{10,... | collective-permute-start | bytes 1769480 | tf_op jit(solution)/shard_map/ppermute | solution.py:37
  13.0 19.9 %collective-permute-start.5 = (f32[384,384]{1,0:T(8,128)}, f32[384,384]{1,0:T(8,128)S(1)}, u32[]{:S(2)}, u32[]{:S(2)}) collective-permute-start(f32[384,384]{1,0:T(8,128)} %bitcast.31), channel_id=1, source_target_pairs={{0,1},{1,0},{2,3},{3,2},{4,5},{5,4},{6,7},{7,6},{8,9},{9,8},{10,11... | collective-permute-start | bytes 1769480 | tf_op jit(solution)/shard_map/ppermute | solution.py:40
  26.5 10.2 %collective-permute-start.3 = (f32[192,384]{1,0:T(8,128)S(1)}, f32[192,384]{1,0:T(8,128)S(1)}, u32[]{:S(2)}, u32[]{:S(2)}) collective-permute-start(f32[192,384]{1,0:T(8,128)S(1)} %slice.20), channel_id=1, source_target_pairs={{0,2},{1,3},{2,4},{3,5},{4,6},{5,7},{6,0},{7,1},{8,10},{9,11},{10,... | collective-permute-start | bytes 884744 | tf_op jit(solution)/shard_map/ppermute | solution.py:37
  26.6 21.0 %collective-permute-start = (s32[2048]{0:T(1024)}, s32[2048]{0:T(1024)S(1)}, u32[]{:S(2)}, u32[]{:S(2)}) collective-permute-start(s32[2048]{0:T(1024)} %bitcast.39), channel_id=1, source_target_pairs={{0,64},{64,0},{1,65},{65,1},{2,66},{66,2},{3,67},{67,3},{4,68},{68... | collective-permute-start | bytes 24584 | tf_op jit(solution)/shard_map/ppermute | solution.py:43
  29.0 10.9 %collective-permute-start.4 = (f32[192,384]{1,0:T(8,128)}, f32[192,384]{1,0:T(8,128)}, u32[]{:S(2)}, u32[]{:S(2)}) collective-permute-start(f32[192,384]{1,0:T(8,128)} %slice.21), channel_id=1, source_target_pairs={{0,6},{1,7},{2,0},{3,1},{4,2},{5,3},{6,4},{7,5},{8,14},{9,15},{10,... | collective-permute-start | bytes 884744 | tf_op jit(solution)/shard_map/ppermute | solution.py:37
  32.9 15.8 %collective-permute-start.6 = (f32[384,384]{1,0:T(8,128)S(1)}, f32[384,384]{1,0:T(8,128)}, u32[]{:S(2)}, u32[]{:S(2)}) collective-permute-start(f32[384,384]{1,0:T(8,128)S(1)} %collective-permute-done.5.refs_6_.rest_4_), channel_id=1, source_target_pairs={{0,2},{1,3},{2,4},{3,5},{4,6},{5,7},{6,0},{7,1},{8,10},{9,11},{10,... | collective-permute-start | bytes 1769480 | tf_op jit(solution)/shard_map/ppermute | solution.py:37
  33.0 17.2 %collective-permute-start.7 = (f32[384,384]{1,0:T(8,128)S(1)}, f32[384,384]{1,0:T(8,128)}, u32[]{:S(2)}, u32[]{:S(2)}) collective-permute-start(f32[384,384]{1,0:T(8,128)S(1)} %collective-permute-done.5.refs_6_.rest_4_), channel_id=1, source_target_pairs={{0,6},{1,7},{2,0},{3,1},{4,2},{5,3},{6,4},{7,5},{8,14},{9,15},{10,... | collective-permute-start | bytes 1769480 | tf_op jit(solution)/shard_map/ppermute | solution.py:37
  40.9 12.4 %collective-permute-start.8 = (f32[384,384]{1,0:T(8,128)S(1)}, f32[384,384]{1,0:T(8,128)}, u32[]{:S(2)}, u32[]{:S(2)}) collective-permute-start(f32[384,384]{1,0:T(8,128)S(1)} %constant_dynamic-update-slice_fusion.refs_5_.rest_3_), channel_id=1, source_target_pairs={{0,1},{1,0},{2,3},{3,2},{4,5},{5,4},{6,7},{7,6},{8,9},{9,8},{10,11... | collective-permute-start | bytes 1769480 | tf_op jit(solution)/shard_map/ppermute | solution.py:40
  53.4 24.7 %collective-permute-start.9 = (f32[256,384]{1,0:T(8,128)}, f32[256,384]{1,0:T(8,128)S(1)}, u32[]{:S(2)}, u32[]{:S(2)}) collective-permute-start(f32[256,384]{1,0:T(8,128)} %get-tuple-element.18._.rest_8_.refs_0_), channel_id=1, source_target_pairs={{0,2},{1,3},{2,4},{3,5},{4,6},{5,7},{6,0},{7,1},{8,10},{9,11},{10,... | collective-permute-start | bytes 1179656 | tf_op jit(solution)/shard_map/ppermute | solution.py:37
  53.6 24.5 %collective-permute-start.10 = (f32[256,384]{1,0:T(8,128)}, f32[256,384]{1,0:T(8,128)S(1)}, u32[]{:S(2)}, u32[]{:S(2)}) collective-permute-start(f32[256,384]{1,0:T(8,128)} %get-tuple-element.18._.rest_8_.refs_0_), channel_id=1, source_target_pairs={{0,6},{1,7},{2,0},{3,1},{4,2},{5,3},{6,4},{7,5},{8,14},{9,15},{10,... | collective-permute-start | bytes 1179656 | tf_op jit(solution)/shard_map/ppermute | solution.py:37
  57.2 20.9 %collective-permute-start.11 = (f32[256,384]{1,0:T(8,128)}, f32[256,384]{1,0:T(8,128)S(1)}, u32[]{:S(2)}, u32[]{:S(2)}) collective-permute-start(f32[256,384]{1,0:T(8,128)} %get-tuple-element.18._.rest_8_.refs_0_), channel_id=1, source_target_pairs={{0,4},{1,5},{2,6},{3,7},{4,0},{5,1},{6,2},{7,3},{8,12},{9,13},{10,... | collective-permute-start | bytes 1179656 | tf_op jit(solution)/shard_map/ppermute | solution.py:37
  58.6 19.5 %collective-permute-start.12 = (f32[256,384]{1,0:T(8,128)}, f32[256,384]{1,0:T(8,128)S(1)}, u32[]{:S(2)}, u32[]{:S(2)}) collective-permute-start(f32[256,384]{1,0:T(8,128)} %get-tuple-element.18._.rest_8_.refs_0_), channel_id=1, source_target_pairs={{0,1},{1,0},{2,3},{3,2},{4,5},{5,4},{6,7},{7,6},{8,9},{9,8},{10,11... | collective-permute-start | bytes 1179656 | tf_op jit(solution)/shard_map/ppermute | solution.py:40
  67.8 10.3 %collective-permute-start.13 = (f32[256,256]{1,0:T(8,128)}, f32[256,256]{1,0:T(8,128)S(1)}, u32[]{:S(2)}, u32[]{:S(2)}) collective-permute-start(f32[256,256]{1,0:T(8,128)} %get-tuple-element.20), channel_id=1, source_target_pairs={{0,64},{64,0},{1,65},{65,1},{2,66},{66,2},{3,67},{67,3},{4,68},{68... | collective-permute-start | bytes 786440 | tf_op jit(solution)/shard_map/ppermute | solution.py:43
  79.9 12.2 %collective-permute-start.14 = (f32[256,384]{1,0:T(8,128)}, f32[256,384]{1,0:T(8,128)S(1)}, u32[]{:S(2)}, u32[]{:S(2)}) collective-permute-start(f32[256,384]{1,0:T(8,128)} %get-tuple-element.26.rest_4_), channel_id=1, source_target_pairs={{0,2},{1,3},{2,4},{3,5},{4,6},{5,7},{6,0},{7,1},{8,10},{9,11},{10,... | collective-permute-start | bytes 1179656 | tf_op jit(solution)/shard_map/ppermute | solution.py:37
  81.3 10.8 %collective-permute-start.15 = (f32[256,384]{1,0:T(8,128)}, f32[256,384]{1,0:T(8,128)S(1)}, u32[]{:S(2)}, u32[]{:S(2)}) collective-permute-start(f32[256,384]{1,0:T(8,128)} %get-tuple-element.26.rest_4_), channel_id=1, source_target_pairs={{0,6},{1,7},{2,0},{3,1},{4,2},{5,3},{6,4},{7,5},{8,14},{9,15},{10,... | collective-permute-start | bytes 1179656 | tf_op jit(solution)/shard_map/ppermute | solution.py:37
  98.6 111.8 %reduce-scatter.2.cloned.1.call-start = ((), (), s32[]{:S(2)}) async-start(), calls=%async_computation.3 | async-start | bytes 5308416 | tf_op jit(solution)/shard_map/reduce_scatter | solution.py:266
  98.7 13.2 %collective-permute-start.17 = (f32[512,256]{1,0:T(8,128)S(1)}, f32[512,256]{1,0:T(8,128)S(1)}, u32[]{:S(2)}, u32[]{:S(2)}) collective-permute-start(f32[512,256]{1,0:T(8,128)S(1)} %copy-done), channel_id=1, source_target_pairs={{0,2},{1,3},{2,4},{3,5},{4,6},{5,7},{6,0},{7,1},{8,10},{9,11},{10,... | collective-permute-start | bytes 1572872 | tf_op jit(solution)/shard_map/ppermute | solution.py:37
  98.9 13.1 %collective-permute-start.18 = (f32[512,256]{1,0:T(8,128)S(1)}, f32[512,256]{1,0:T(8,128)S(1)}, u32[]{:S(2)}, u32[]{:S(2)}) collective-permute-start(f32[512,256]{1,0:T(8,128)S(1)} %copy-done), channel_id=1, source_target_pairs={{0,6},{1,7},{2,0},{3,1},{4,2},{5,3},{6,4},{7,5},{8,14},{9,15},{10,... | collective-permute-start | bytes 1572872 | tf_op jit(solution)/shard_map/ppermute | solution.py:37
  102.0 13.4 %collective-permute-start.21 = (f32[512,256]{1,0:T(8,128)S(1)}, f32[512,256]{1,0:T(8,128)S(1)}, u32[]{:S(2)}, u32[]{:S(2)}) collective-permute-start(f32[512,256]{1,0:T(8,128)S(1)} %copy-done), channel_id=1, source_target_pairs={{0,1},{1,0},{2,3},{3,2},{4,5},{5,4},{6,7},{7,6},{8,9},{9,8},{10,11... | collective-permute-start | bytes 1572872 | tf_op jit(solution)/shard_map/ppermute | solution.py:40
  115.4 10.6 %collective-permute-start.22 = (f32[512,256]{1,0:T(8,128)S(1)}, f32[512,256]{1,0:T(8,128)S(1)}, u32[]{:S(2)}, u32[]{:S(2)}) collective-permute-start(f32[512,256]{1,0:T(8,128)S(1)} %collective-permute-done.21.rest_5_.refs_6_), channel_id=1, source_target_pairs={{0,2},{1,3},{2,4},{3,5},{4,6},{5,7},{6,0},{7,1},{8,10},{9,11},{10,... | collective-permute-start | bytes 1572872 | tf_op jit(solution)/shard_map/ppermute | solution.py:37
  115.4 10.6 %collective-permute-start.23 = (f32[512,256]{1,0:T(8,128)S(1)}, f32[512,256]{1,0:T(8,128)S(1)}, u32[]{:S(2)}, u32[]{:S(2)}) collective-permute-start(f32[512,256]{1,0:T(8,128)S(1)} %collective-permute-done.21.rest_5_.refs_6_), channel_id=1, source_target_pairs={{0,6},{1,7},{2,0},{3,1},{4,2},{5,3},{6,4},{7,5},{8,14},{9,15},{10,... | collective-permute-start | bytes 1572872 | tf_op jit(solution)/shard_map/ppermute | solution.py:37
  120.4 11.6 %collective-permute-start.24 = (f32[512,256]{1,0:T(8,128)S(1)}, f32[512,256]{1,0:T(8,128)}, u32[]{:S(2)}, u32[]{:S(2)}) collective-permute-start(f32[512,256]{1,0:T(8,128)S(1)} %constant_dynamic-update-slice_fusion.2.rest_4_.refs_5_), channel_id=1, source_target_pairs={{0,1},{1,0},{2,3},{3,2},{4,5},{5,4},{6,7},{7,6},{8,9},{9,8},{10,11... | collective-permute-start | bytes 1572872 | tf_op jit(solution)/shard_map/ppermute | solution.py:40
  132.1 16.9 %collective-permute-start.25 = (f32[384,256]{1,0:T(8,128)}, f32[384,256]{1,0:T(8,128)S(1)}, u32[]{:S(2)}, u32[]{:S(2)}) collective-permute-start(f32[384,256]{1,0:T(8,128)} %get-tuple-element.30.rest_0_), channel_id=1, source_target_pairs={{0,1},{1,0},{2,3},{3,2},{4,5},{5,4},{6,7},{7,6},{8,9},{9,8},{10,11... | collective-permute-start | bytes 1179656 | tf_op jit(solution)/shard_map/ppermute | solution.py:40
  133.1 19.3 %collective-permute-start.28 = (f32[384,256]{1,0:T(8,128)}, f32[384,256]{1,0:T(8,128)S(1)}, u32[]{:S(2)}, u32[]{:S(2)}) collective-permute-start(f32[384,256]{1,0:T(8,128)} %get-tuple-element.30.rest_0_), channel_id=1, source_target_pairs={{0,4},{1,5},{2,6},{3,7},{4,0},{5,1},{6,2},{7,3},{8,12},{9,13},{10,... | collective-permute-start | bytes 1179656 | tf_op jit(solution)/shard_map/ppermute | solution.py:37
  134.7 19.8 %collective-permute-start.30 = (f32[384,256]{1,0:T(8,128)}, f32[384,256]{1,0:T(8,128)S(1)}, u32[]{:S(2)}, u32[]{:S(2)}) collective-permute-start(f32[384,256]{1,0:T(8,128)} %get-tuple-element.30.rest_0_), channel_id=1, source_target_pairs={{0,2},{1,3},{2,4},{3,5},{4,6},{5,7},{6,0},{7,1},{8,10},{9,11},{10,... | collective-permute-start | bytes 1179656 | tf_op jit(solution)/shard_map/ppermute | solution.py:37
  137.3 17.2 %collective-permute-start.31 = (f32[384,256]{1,0:T(8,128)}, f32[384,256]{1,0:T(8,128)S(1)}, u32[]{:S(2)}, u32[]{:S(2)}) collective-permute-start(f32[384,256]{1,0:T(8,128)} %get-tuple-element.30.rest_0_), channel_id=1, source_target_pairs={{0,6},{1,7},{2,0},{3,1},{4,2},{5,3},{6,4},{7,5},{8,14},{9,15},{10,... | collective-permute-start | bytes 1179656 | tf_op jit(solution)/shard_map/ppermute | solution.py:37
  149.1 12.4 %collective-permute-start.26 = (f32[384,256]{1,0:T(8,128)S(1)}, f32[384,256]{1,0:T(8,128)S(1)}, u32[]{:S(2)}, u32[]{:S(2)}) collective-permute-start(f32[384,256]{1,0:T(8,128)S(1)} %collective-permute-done.25.rest_4_), channel_id=1, source_target_pairs={{0,2},{1,3},{2,4},{3,5},{4,6},{5,7},{6,0},{7,1},{8,10},{9,11},{10,... | collective-permute-start | bytes 1179656 | tf_op jit(solution)/shard_map/ppermute | solution.py:37
  150.6 10.9 %collective-permute-start.27 = (f32[384,256]{1,0:T(8,128)S(1)}, f32[384,256]{1,0:T(8,128)S(1)}, u32[]{:S(2)}, u32[]{:S(2)}) collective-permute-start(f32[384,256]{1,0:T(8,128)S(1)} %collective-permute-done.25.rest_4_), channel_id=1, source_target_pairs={{0,6},{1,7},{2,0},{3,1},{4,2},{5,3},{6,4},{7,5},{8,14},{9,15},{10,... | collective-permute-start | bytes 1179656 | tf_op jit(solution)/shard_map/ppermute | solution.py:37
  (35 other events, 328.5 us)
Sparse Core Ops, SparseCore 0:
  9.7 34.5 all-gather.4
  46.0 34.2 all-gather.8
  98.7 26.8 all-gather.6
  168.1 42.2 reduce-scatter.1

commit v4 on v3

--- a/solution.py
+++ b/solution.py
@@ -257,9 +257,8 @@
         coupling_kernel, array(BAND, WIDE), [place, row[None], live_rows], [], [update_rows] + picked_all,
         [((SIDE, WIDE, BAND), f32), ((ROOT, BAND), f32), ((BAND, BAND), f32)], 16, 12,
     )
-    update_near = near_col(flipped)
-
-    update_rest = rest_col(*update_near[3:])
+    update_all = gather_col(flipped)
+    update_near, update_rest = update_all[:5], update_all[5:]
     total = partial(0, update_near, cols, coupling, gram)
     (total,) = hold([total], update_rest)
     total = partial(5, update_rest, cols, coupling, gram, total)

time: 217 us -> 221 us (1.018)
  waiting for transfers between devices: 82.6 us -> 85.3 us
  starting transfers between devices: 56.7 us -> 59.1 us
    ppermute x22 -> x23, waiting for transfers between devices: 28.8 us -> 35.2 us  [shift(): lax.ppermute(x, axis, [(i, (i // 2 + step) % 4 * 2 + i % 2) for i in rang...]
    reduce_scatter x1, waiting for transfers between devices: 42.4 us -> 38 us  [per_device(): separator = lax.psum_scatter(total, 'row', scatter_dimension=0, tiled=True)]
    ppermute x22 -> x23, starting transfers between devices: 37.3 us -> 39.2 us  [shift(): lax.ppermute(x, axis, [(i, (i // 2 + step) % 4 * 2 + i % 2) for i in rang...]
    unnamed x66 -> x67, local copies, waits for them, and re-layouts: 5.43 us -> 4 us
  transfers between devices with their start and end apart: 36 -> 37, of which waited for: 13 -> 14; matrix products, arithmetic and copies ran while one was open for 5% -> 5% of each run, Pallas kernels for 17% -> 17%
where the time goes in v4:
time: 221 us
  waiting for transfers between devices  85.3 us (39%)
  starting transfers between devices  59.1 us (27%)
  Pallas kernels  47.4 us (21%)
  between operations  15 us (7%)
  local copies, waits for them, and re-layouts  8.7 us (4%)
  other arithmetic  5.15 us (2%)
    ppermute x23, starting transfers between devices, shift(): lax.ppermute(x, axis, [(i, (i // 2 + step) % 4 * 2 + i % 2) for i in rang...  39.2 us
    reduce_scatter x1, waiting for transfers between devices, per_device(): separator = lax.psum_scatter(total, 'row', scatter_dimension=0, tiled=True)  38 us
    pallas_call x5, Pallas kernels, call(): pl.pallas_call(kernel, out_shape=out, in_specs=[SMEM] * len(scalars) + [V...  36.6 us
    ppermute x23, waiting for transfers between devices, shift(): lax.ppermute(x, axis, [(i, (i // 2 + step) % 4 * 2 + i % 2) for i in rang...  35.2 us
    ppermute x8, starting transfers between devices, swap(): return lax.ppermute(x, axis, [(i, i ^ 1) for i in range(SIDE)])  18 us
    pallas_call x2, Pallas kernels, partial(): pl.pallas_call(functools.partial(partial_kernel, first, count), out_shape...  10.8 us
    ppermute x8, waiting for transfers between devices, swap(): return lax.ppermute(x, axis, [(i, i ^ 1) for i in range(SIDE)])  10.7 us
  transfers between devices with their start and end apart: 37, of which 14 were waited for; matrix products, arithmetic and copies ran while one was open for 5% of the time, Pallas kernels for 17%

profile of v4, /device:TPU:0, one launch (start us, length us, event | category | flops | bytes accessed | tf_op | source)
XLA Modules:
  0.0 220.5 jit_solution(6536564839284424271)
XLA Ops:
  8.7 2.1 collective-permute-start.1
  10.8 2.2 collective-permute-start.2
  13.0 3.2 %collective-permute-start.5 = (f32[384,384]{1,0:T(8,128)}, f32[384,384]{1,0:T(8,128)S(1)}, u32[]{:S(2)}, u32[]{:S(2)}) collective-permute-start(f32[384,384]{1,0:T(8,128)} %bitcast.31), channel_id=1, source_target_pairs={{0,1},{1,0},{2,3},{3,2},{4,5},{5,4},{6,7},{7,6},{8,9},{9,8},{10,11... | collective-permute-start | bytes 1769480 | tf_op jit(solution)/shard_map/ppermute | solution.py:40
  16.2 10.3 %collective-permute-done.1.refs_3_.rest_1_ = f32[384,384]{1,0:T(8,128)S(1)} collective-permute-done((f32[384,384]{1,0:T(8,128)}, f32[384,384]{1,0:T(8,128)S(1)}, u32[]{:S(2)}, u32[]{:S(2)}) %collective-permute-start.1) | collective-permute-done | bytes 589856 | tf_op jit(solution)/shard_map/ppermute | solution.py:37
  29.0 3.1 %collective-permute-start.4 = (f32[192,384]{1,0:T(8,128)}, f32[192,384]{1,0:T(8,128)}, u32[]{:S(2)}, u32[]{:S(2)}) collective-permute-start(f32[192,384]{1,0:T(8,128)} %slice.29), channel_id=1, source_target_pairs={{0,6},{1,7},{2,0},{3,1},{4,2},{5,3},{6,4},{7,5},{8,14},{9,15},{10,... | collective-permute-start | bytes 884744 | tf_op jit(solution)/shard_map/ppermute | solution.py:37
  33.0 3.2 %collective-permute-start.7 = (f32[384,384]{1,0:T(8,128)S(1)}, f32[384,384]{1,0:T(8,128)}, u32[]{:S(2)}, u32[]{:S(2)}) collective-permute-start(f32[384,384]{1,0:T(8,128)S(1)} %collective-permute-done.5.refs_6_.rest_4_), channel_id=1, source_target_pairs={{0,6},{1,7},{2,0},{3,1},{4,2},{5,3},{6,4},{7,5},{8,14},{9,15},{10,... | collective-permute-start | bytes 1769480 | tf_op jit(solution)/shard_map/ppermute | solution.py:37
  36.7 3.3 %collective-permute-done.4 = f32[192,384]{1,0:T(8,128)} collective-permute-done((f32[192,384]{1,0:T(8,128)}, f32[192,384]{1,0:T(8,128)}, u32[]{:S(2)}, u32[]{:S(2)}) %collective-permute-start.4) | collective-permute-done | bytes 294944 | tf_op jit(solution)/shard_map/ppermute | solution.py:37
  40.9 3.0 %collective-permute-start.8 = (f32[384,384]{1,0:T(8,128)S(1)}, f32[384,384]{1,0:T(8,128)}, u32[]{:S(2)}, u32[]{:S(2)}) collective-permute-start(f32[384,384]{1,0:T(8,128)S(1)} %constant_dynamic-update-slice_fusion.refs_5_.rest_3_), channel_id=1, source_target_pairs={{0,1},{1,0},{2,3},{3,2},{4,5},{5,4},{6,7},{7,6},{8,9},{9,8},{10,11... | collective-permute-start | bytes 1769480 | tf_op jit(solution)/shard_map/ppermute | solution.py:40
  50.1 3.2 %collective-permute-done.8.refs_9_.rest_7_ = f32[384,384]{1,0:T(8,128)} collective-permute-done((f32[384,384]{1,0:T(8,128)S(1)}, f32[384,384]{1,0:T(8,128)}, u32[]{:S(2)}, u32[]{:S(2)}) %collective-permute-start.8) | collective-permute-done | bytes 589856 | tf_op jit(solution)/shard_map/ppermute | solution.py:40
  53.6 3.6 %collective-permute-start.10 = (f32[256,384]{1,0:T(8,128)}, f32[256,384]{1,0:T(8,128)S(1)}, u32[]{:S(2)}, u32[]{:S(2)}) collective-permute-start(f32[256,384]{1,0:T(8,128)} %get-tuple-element.18._.rest_8_.refs_0_), channel_id=1, source_target_pairs={{0,6},{1,7},{2,0},{3,1},{4,2},{5,3},{6,4},{7,5},{8,14},{9,15},{10,... | collective-permute-start | bytes 1179656 | tf_op jit(solution)/shard_map/ppermute | solution.py:37
  58.6 2.9 %collective-permute-start.12 = (f32[256,384]{1,0:T(8,128)}, f32[256,384]{1,0:T(8,128)S(1)}, u32[]{:S(2)}, u32[]{:S(2)}) collective-permute-start(f32[256,384]{1,0:T(8,128)} %get-tuple-element.18._.rest_8_.refs_0_), channel_id=1, source_target_pairs={{0,1},{1,0},{2,3},{3,2},{4,5},{5,4},{6,7},{7,6},{8,9},{9,8},{10,11... | collective-permute-start | bytes 1179656 | tf_op jit(solution)/shard_map/ppermute | solution.py:40
  62.8 5.0 %shard_map.78 = (f32[256,256]{1,0:T(8,128)}, f32[256,256]{1,0:T(8,128)}) custom-call(s32[512]{0:T(512)} %pad_add_fusion.place, f32[4096,256]{1,0:T(8,128)} %all-gather.5.cloned.1.call-done.root, f32[256,384]{1,0:T(8,128)} %get-tuple-element.18._.rest_8_.refs_0_), custom_call_target="tpu_custom_call" | custom-call | flops 5000000000 | bytes 15000000 | tf_op jit(solution)/shard_map/pallas_call | solution.py:85
  67.9 10.1 %shard_map.79.refs_5_ = f32[8,384,384]{2,1,0:T(8,128)} custom-call(f32[384,384]{1,0:T(8,128)} %bitcast.33, f32[384,384]{1,0:T(8,128)} %bitcast.34, f32[384,384]{1,0:T(8,128)} %copy-done.4, f32[384,384]{1,0:T(8,128)} %copy-done.5, f32[384,384]{1,0:T(8,128)} %copy-done.6, f32[384,384]{1,0:T(8,128)} %copy-done.11, ...), custom_call_target="tpu_custom_call" | custom-call | flops 12000000000 | bytes 36000000 | tf_op jit(solution)/shard_map/pallas_call | solution.py:85
  84.9 1.8 pad_maximum_fusion.refs_0_
  86.7 5.5 %shard_map.81.refs_1_ = f32[256,384]{1,0:T(8,128)} custom-call(s32[5]{0:T(128)} %stack.40.cols, f32[256,384]{1,0:T(8,128)} %get-tuple-element.22.rest_0_, f32[256,384]{1,0:T(8,128)} %get-tuple-element.23.rest_1_, f32[256,384]{1,0:T(8,128)} %get-tuple-element.24.rest_2_, f32[256,384]{1,0:T(8,128)} %get-tuple-element.25.rest_3_, ...), custom_call_target="tpu_custom_call" | custom-call | flops 5000000000 | bytes 15000000 | tf_op jit(solution)/shard_map/pallas_call | solution.py:85
  93.9 4.8 %shard_map.83.refs_0_ = f32[384,256]{1,0:T(8,128)} custom-call(s32[3]{0:T(128)} %pad_add_fusion.1.cols, s32[1]{0:T(128)} %bitcast.1.row, s32[1]{0:T(128)S(6)} %copy.46.live, f32[256,384]{1,0:T(8,128)} %get-tuple-element.27.part, f32[256,384]{1,0:T(8,128)} %copy-done.15, f32[256,384]{1,0:T(8,128)} %copy-done.16, f32[256,384]{1,0:T(8,128)} %copy-done.17, ...), custom_call_target="tpu_custom_call" | custom-call | flops 3000000000 | bytes 9000000 | tf_op jit(solution)/shard_map/pallas_call | solution.py:85
  99.0 3.1 %collective-permute-start.18 = (f32[512,256]{1,0:T(8,128)S(1)}, f32[512,256]{1,0:T(8,128)S(1)}, u32[]{:S(2)}, u32[]{:S(2)}) collective-permute-start(f32[512,256]{1,0:T(8,128)S(1)} %copy-done), channel_id=1, source_target_pairs={{0,6},{1,7},{2,0},{3,1},{4,2},{5,3},{6,4},{7,5},{8,14},{9,15},{10,... | collective-permute-start | bytes 1572872 | tf_op jit(solution)/shard_map/ppermute | solution.py:37
  102.1 1.8 collective-permute-start.21
  104.0 8.2 %collective-permute-done.17.rest_2_.refs_3_ = f32[512,256]{1,0:T(8,128)S(1)} collective-permute-done((f32[512,256]{1,0:T(8,128)S(1)}, f32[512,256]{1,0:T(8,128)S(1)}, u32[]{:S(2)}, u32[]{:S(2)}) %collective-permute-start.17) | collective-permute-done | bytes 524320 | tf_op jit(solution)/shard_map/ppermute | solution.py:37
  112.3 3.3 %collective-permute-start.20 = (f32[256,256]{1,0:T(8,128)S(1)}, f32[256,256]{1,0:T(8,128)S(1)}, u32[]{:S(2)}, u32[]{:S(2)}) collective-permute-start(f32[256,256]{1,0:T(8,128)S(1)} %slice.31), channel_id=1, source_target_pairs={{0,6},{1,7},{2,0},{3,1},{4,2},{5,3},{6,4},{7,5},{8,14},{9,15},{10,... | collective-permute-start | bytes 786440 | tf_op jit(solution)/shard_map/ppermute | solution.py:37
  115.7 3.2 %collective-permute-start.23 = (f32[512,256]{1,0:T(8,128)S(1)}, f32[512,256]{1,0:T(8,128)S(1)}, u32[]{:S(2)}, u32[]{:S(2)}) collective-permute-start(f32[512,256]{1,0:T(8,128)S(1)} %collective-permute-done.21.rest_5_.refs_6_), channel_id=1, source_target_pairs={{0,6},{1,7},{2,0},{3,1},{4,2},{5,3},{6,4},{7,5},{8,14},{9,15},{10,... | collective-permute-start | bytes 1572872 | tf_op jit(solution)/shard_map/ppermute | solution.py:37
  122.3 3.8 %collective-permute-done.22.rest_6_.refs_7_ = f32[512,256]{1,0:T(8,128)S(1)} collective-permute-done((f32[512,256]{1,0:T(8,128)S(1)}, f32[512,256]{1,0:T(8,128)S(1)}, u32[]{:S(2)}, u32[]{:S(2)}) %collective-permute-start.22) | collective-permute-done | bytes 524320 | tf_op jit(solution)/shard_map/ppermute | solution.py:37
  126.1 5.3 %collective-permute-done.24.rest_8_.refs_9_ = f32[512,256]{1,0:T(8,128)} collective-permute-done((f32[512,256]{1,0:T(8,128)S(1)}, f32[512,256]{1,0:T(8,128)}, u32[]{:S(2)}, u32[]{:S(2)}) %collective-permute-start.24) | collective-permute-done | bytes 524320 | tf_op jit(solution)/shard_map/ppermute | solution.py:40
  131.7 3.2 %collective-permute-start.30 = (f32[384,256]{1,0:T(8,128)}, f32[384,256]{1,0:T(8,128)S(1)}, u32[]{:S(2)}, u32[]{:S(2)}) collective-permute-start(f32[384,256]{1,0:T(8,128)} %get-tuple-element.30.rest_0_), channel_id=1, source_target_pairs={{0,6},{1,7},{2,0},{3,1},{4,2},{5,3},{6,4},{7,5},{8,14},{9,15},{10,... | collective-permute-start | bytes 1179656 | tf_op jit(solution)/shard_map/ppermute | solution.py:37
  136.2 1.8 collective-permute-start.25
  138.0 4.9 %collective-permute-done.28.rest_1_ = f32[384,256]{1,0:T(8,128)S(1)} collective-permute-done((f32[384,256]{1,0:T(8,128)}, f32[384,256]{1,0:T(8,128)S(1)}, u32[]{:S(2)}, u32[]{:S(2)}) %collective-permute-start.28) | collective-permute-done | bytes 393248 | tf_op jit(solution)/shard_map/ppermute | solution.py:37
  143.0 3.3 %collective-permute-start.31 = (f32[192,256]{1,0:T(8,128)S(1)}, f32[192,256]{1,0:T(8,128)S(1)}, u32[]{:S(2)}, u32[]{:S(2)}) collective-permute-start(f32[192,256]{1,0:T(8,128)S(1)} %slice.33), channel_id=1, source_target_pairs={{0,6},{1,7},{2,0},{3,1},{4,2},{5,3},{6,4},{7,5},{8,14},{9,15},{10,... | collective-permute-start | bytes 589832 | tf_op jit(solution)/shard_map/ppermute | solution.py:37
  146.3 11.1 %shard_map.84.coupling = f32[256,384]{1,0:T(8,128)} custom-call(s32[2048]{0:T(1024)} %fusion.8.place, s32[1]{0:T(128)} %bitcast.1.row, s32[1]{0:T(128)S(6)} %copy.46.live, f32[3072,256]{1,0:T(8,128)} %all-gather.7.cloned.1.call-done.rest_0_, f32[512,256]{1,0:T(8,128)} %get-tuple-element.28.rest_1_.refs_2_, f32[512,256]{1,0:T(8,128)} %copy-done.7, ...), custom_call_target="tpu_custom_call" | custom-call | flops 12000000000 | bytes 36000000 | tf_op jit(solution)/shard_map/pallas_call | solution.py:85
  157.5 3.2 %collective-permute-start.27 = (f32[384,256]{1,0:T(8,128)S(1)}, f32[384,256]{1,0:T(8,128)S(1)}, u32[]{:S(2)}, u32[]{:S(2)}) collective-permute-start(f32[384,256]{1,0:T(8,128)S(1)} %collective-permute-done.25.rest_4_), channel_id=1, source_target_pairs={{0,6},{1,7},{2,0},{3,1},{4,2},{5,3},{6,4},{7,5},{8,14},{9,15},{10,... | collective-permute-start | bytes 1179656 | tf_op jit(solution)/shard_map/ppermute | solution.py:37
  162.6 6.0 %shard_map.86.refs_0_ = f32[3072,384]{1,0:T(8,128)} custom-call(s32[8]{0:T(128)} %stack.41.cols, f32[256,384]{1,0:T(8,128)} %shard_map.84.coupling, f32[384,256]{1,0:T(8,128)} %get-tuple-element.30.rest_0_, f32[384,256]{1,0:T(8,128)} %copy-done.24, f32[384,256]{1,0:T(8,128)} %copy-done.25, f32[384,256]{1,0:T(8,128)} %copy-done.26, f32[384,256]{1,0:T(8,128)} %copy-done.30, ...), custom_call_target="tpu_custom_call" | custom-call | flops 5000000000 | bytes 15000000 | tf_op jit(solution)/shard_map/pallas_call | solution.py:197
  171.2 4.8 %shard_map.88 = f32[3072,384]{1,0:T(8,128)} custom-call(s32[8]{0:T(128)} %stack.41.cols, f32[256,384]{1,0:T(8,128)} %shard_map.84.coupling, f32[384,256]{1,0:T(8,128)} %copy-done.1, f32[384,256]{1,0:T(8,128)} %copy-done.2, f32[384,256]{1,0:T(8,128)} %copy-done.3, f32[8,384,384]{2,1,0:T(8,128)} %get-tuple-element.31.rest_5_.rest_3_, ...), custom_call_target="tpu_custom_call", output_to_operand_aliasing={{}: (6, {})} | custom-call | flops 3000000000 | bytes 9000000 | tf_op jit(solution)/shard_map/pallas_call | solution.py:197
  176.0 38.0 %reduce-scatter.2.cloned.1.call-done = f32[384,384]{1,0:T(8,128)} async-done(((f32[3072,384]{1,0:T(8,128)}), f32[384,384]{1,0:T(8,128)}) %reduce-scatter.2.cloned.1.call-update) | async-done | bytes 589840 | tf_op jit(solution)/shard_map/reduce_scatter | solution.py:265
  (147 shorter events, 33.1 us)
Async XLA Ops:
  7.2 55.6 %all-gather.5.cloned.1.call-start = ((), (), s32[]{:S(2)}) async-start(), calls=%async_computation.1 | async-start | bytes 4718592 | tf_op jit(solution)/shard_map/all_gather | solution.py:220
  7.9 78.7 %all-gather.9.cloned.1.call-start = ((), (), s32[]{:S(2)}) async-start(), calls=%async_computation.4 | async-start | bytes 5308416 | tf_op jit(solution)/shard_map/all_gather | solution.py:222
  8.7 122.8 %all-gather.7.cloned.1.call-start = ((), (), s32[]{:S(2)}) async-start(), calls=%async_computation.2 | async-start | bytes 3538944 | tf_op jit(solution)/shard_map/all_gather | solution.py:250
  8.7 17.7 %collective-permute-start.1 = (f32[384,384]{1,0:T(8,128)}, f32[384,384]{1,0:T(8,128)S(1)}, u32[]{:S(2)}, u32[]{:S(2)}) collective-permute-start(f32[384,384]{1,0:T(8,128)} %bitcast.29), channel_id=1, source_target_pairs={{0,2},{1,3},{2,4},{3,5},{4,6},{5,7},{6,0},{7,1},{8,10},{9,11},{10,... | collective-permute-start | bytes 1769480 | tf_op jit(solution)/shard_map/ppermute | solution.py:37
  10.8 17.4 %collective-permute-start.2 = (f32[384,384]{1,0:T(8,128)}, f32[384,384]{1,0:T(8,128)S(1)}, u32[]{:S(2)}, u32[]{:S(2)}) collective-permute-start(f32[384,384]{1,0:T(8,128)} %bitcast.30), channel_id=1, source_target_pairs={{0,6},{1,7},{2,0},{3,1},{4,2},{5,3},{6,4},{7,5},{8,14},{9,15},{10,... | collective-permute-start | bytes 1769480 | tf_op jit(solution)/shard_map/ppermute | solution.py:37
  13.0 19.9 %collective-permute-start.5 = (f32[384,384]{1,0:T(8,128)}, f32[384,384]{1,0:T(8,128)S(1)}, u32[]{:S(2)}, u32[]{:S(2)}) collective-permute-start(f32[384,384]{1,0:T(8,128)} %bitcast.31), channel_id=1, source_target_pairs={{0,1},{1,0},{2,3},{3,2},{4,5},{5,4},{6,7},{7,6},{8,9},{9,8},{10,11... | collective-permute-start | bytes 1769480 | tf_op jit(solution)/shard_map/ppermute | solution.py:40
  26.6 20.9 %collective-permute-start = (s32[2048]{0:T(1024)}, s32[2048]{0:T(1024)S(1)}, u32[]{:S(2)}, u32[]{:S(2)}) collective-permute-start(s32[2048]{0:T(1024)} %bitcast.39), channel_id=1, source_target_pairs={{0,64},{64,0},{1,65},{65,1},{2,66},{66,2},{3,67},{67,3},{4,68},{68... | collective-permute-start | bytes 24584 | tf_op jit(solution)/shard_map/ppermute | solution.py:43
  29.0 10.9 %collective-permute-start.4 = (f32[192,384]{1,0:T(8,128)}, f32[192,384]{1,0:T(8,128)}, u32[]{:S(2)}, u32[]{:S(2)}) collective-permute-start(f32[192,384]{1,0:T(8,128)} %slice.29), channel_id=1, source_target_pairs={{0,6},{1,7},{2,0},{3,1},{4,2},{5,3},{6,4},{7,5},{8,14},{9,15},{10,... | collective-permute-start | bytes 884744 | tf_op jit(solution)/shard_map/ppermute | solution.py:37
  32.9 15.8 %collective-permute-start.6 = (f32[384,384]{1,0:T(8,128)S(1)}, f32[384,384]{1,0:T(8,128)}, u32[]{:S(2)}, u32[]{:S(2)}) collective-permute-start(f32[384,384]{1,0:T(8,128)S(1)} %collective-permute-done.5.refs_6_.rest_4_), channel_id=1, source_target_pairs={{0,2},{1,3},{2,4},{3,5},{4,6},{5,7},{6,0},{7,1},{8,10},{9,11},{10,... | collective-permute-start | bytes 1769480 | tf_op jit(solution)/shard_map/ppermute | solution.py:37
  33.0 17.2 %collective-permute-start.7 = (f32[384,384]{1,0:T(8,128)S(1)}, f32[384,384]{1,0:T(8,128)}, u32[]{:S(2)}, u32[]{:S(2)}) collective-permute-start(f32[384,384]{1,0:T(8,128)S(1)} %collective-permute-done.5.refs_6_.rest_4_), channel_id=1, source_target_pairs={{0,6},{1,7},{2,0},{3,1},{4,2},{5,3},{6,4},{7,5},{8,14},{9,15},{10,... | collective-permute-start | bytes 1769480 | tf_op jit(solution)/shard_map/ppermute | solution.py:37
  40.9 12.4 %collective-permute-start.8 = (f32[384,384]{1,0:T(8,128)S(1)}, f32[384,384]{1,0:T(8,128)}, u32[]{:S(2)}, u32[]{:S(2)}) collective-permute-start(f32[384,384]{1,0:T(8,128)S(1)} %constant_dynamic-update-slice_fusion.refs_5_.rest_3_), channel_id=1, source_target_pairs={{0,1},{1,0},{2,3},{3,2},{4,5},{5,4},{6,7},{7,6},{8,9},{9,8},{10,11... | collective-permute-start | bytes 1769480 | tf_op jit(solution)/shard_map/ppermute | solution.py:40
  53.4 24.7 %collective-permute-start.9 = (f32[256,384]{1,0:T(8,128)}, f32[256,384]{1,0:T(8,128)S(1)}, u32[]{:S(2)}, u32[]{:S(2)}) collective-permute-start(f32[256,384]{1,0:T(8,128)} %get-tuple-element.18._.rest_8_.refs_0_), channel_id=1, source_target_pairs={{0,2},{1,3},{2,4},{3,5},{4,6},{5,7},{6,0},{7,1},{8,10},{9,11},{10,... | collective-permute-start | bytes 1179656 | tf_op jit(solution)/shard_map/ppermute | solution.py:37
  53.6 24.5 %collective-permute-start.10 = (f32[256,384]{1,0:T(8,128)}, f32[256,384]{1,0:T(8,128)S(1)}, u32[]{:S(2)}, u32[]{:S(2)}) collective-permute-start(f32[256,384]{1,0:T(8,128)} %get-tuple-element.18._.rest_8_.refs_0_), channel_id=1, source_target_pairs={{0,6},{1,7},{2,0},{3,1},{4,2},{5,3},{6,4},{7,5},{8,14},{9,15},{10,... | collective-permute-start | bytes 1179656 | tf_op jit(solution)/shard_map/ppermute | solution.py:37
  57.2 20.9 %collective-permute-start.11 = (f32[256,384]{1,0:T(8,128)}, f32[256,384]{1,0:T(8,128)S(1)}, u32[]{:S(2)}, u32[]{:S(2)}) collective-permute-start(f32[256,384]{1,0:T(8,128)} %get-tuple-element.18._.rest_8_.refs_0_), channel_id=1, source_target_pairs={{0,4},{1,5},{2,6},{3,7},{4,0},{5,1},{6,2},{7,3},{8,12},{9,13},{10,... | collective-permute-start | bytes 1179656 | tf_op jit(solution)/shard_map/ppermute | solution.py:37
  58.6 19.5 %collective-permute-start.12 = (f32[256,384]{1,0:T(8,128)}, f32[256,384]{1,0:T(8,128)S(1)}, u32[]{:S(2)}, u32[]{:S(2)}) collective-permute-start(f32[256,384]{1,0:T(8,128)} %get-tuple-element.18._.rest_8_.refs_0_), channel_id=1, source_target_pairs={{0,1},{1,0},{2,3},{3,2},{4,5},{5,4},{6,7},{7,6},{8,9},{9,8},{10,11... | collective-permute-start | bytes 1179656 | tf_op jit(solution)/shard_map/ppermute | solution.py:40
  67.8 10.4 %collective-permute-start.13 = (f32[256,256]{1,0:T(8,128)}, f32[256,256]{1,0:T(8,128)S(1)}, u32[]{:S(2)}, u32[]{:S(2)}) collective-permute-start(f32[256,256]{1,0:T(8,128)} %get-tuple-element.20), channel_id=1, source_target_pairs={{0,64},{64,0},{1,65},{65,1},{2,66},{66,2},{3,67},{67,3},{4,68},{68... | collective-permute-start | bytes 786440 | tf_op jit(solution)/shard_map/ppermute | solution.py:43
  80.0 12.2 %collective-permute-start.14 = (f32[256,384]{1,0:T(8,128)}, f32[256,384]{1,0:T(8,128)S(1)}, u32[]{:S(2)}, u32[]{:S(2)}) collective-permute-start(f32[256,384]{1,0:T(8,128)} %get-tuple-element.26.rest_4_), channel_id=1, source_target_pairs={{0,2},{1,3},{2,4},{3,5},{4,6},{5,7},{6,0},{7,1},{8,10},{9,11},{10,... | collective-permute-start | bytes 1179656 | tf_op jit(solution)/shard_map/ppermute | solution.py:37
  81.5 10.8 %collective-permute-start.15 = (f32[256,384]{1,0:T(8,128)}, f32[256,384]{1,0:T(8,128)S(1)}, u32[]{:S(2)}, u32[]{:S(2)}) collective-permute-start(f32[256,384]{1,0:T(8,128)} %get-tuple-element.26.rest_4_), channel_id=1, source_target_pairs={{0,6},{1,7},{2,0},{3,1},{4,2},{5,3},{6,4},{7,5},{8,14},{9,15},{10,... | collective-permute-start | bytes 1179656 | tf_op jit(solution)/shard_map/ppermute | solution.py:37
  98.8 115.3 %reduce-scatter.2.cloned.1.call-start = ((), (), s32[]{:S(2)}) async-start(), calls=%async_computation.3 | async-start | bytes 5308416 | tf_op jit(solution)/shard_map/reduce_scatter | solution.py:265
  98.8 13.4 %collective-permute-start.17 = (f32[512,256]{1,0:T(8,128)S(1)}, f32[512,256]{1,0:T(8,128)S(1)}, u32[]{:S(2)}, u32[]{:S(2)}) collective-permute-start(f32[512,256]{1,0:T(8,128)S(1)} %copy-done), channel_id=1, source_target_pairs={{0,2},{1,3},{2,4},{3,5},{4,6},{5,7},{6,0},{7,1},{8,10},{9,11},{10,... | collective-permute-start | bytes 1572872 | tf_op jit(solution)/shard_map/ppermute | solution.py:37
  99.0 13.3 %collective-permute-start.18 = (f32[512,256]{1,0:T(8,128)S(1)}, f32[512,256]{1,0:T(8,128)S(1)}, u32[]{:S(2)}, u32[]{:S(2)}) collective-permute-start(f32[512,256]{1,0:T(8,128)S(1)} %copy-done), channel_id=1, source_target_pairs={{0,6},{1,7},{2,0},{3,1},{4,2},{5,3},{6,4},{7,5},{8,14},{9,15},{10,... | collective-permute-start | bytes 1572872 | tf_op jit(solution)/shard_map/ppermute | solution.py:37
  102.1 13.6 %collective-permute-start.21 = (f32[512,256]{1,0:T(8,128)S(1)}, f32[512,256]{1,0:T(8,128)S(1)}, u32[]{:S(2)}, u32[]{:S(2)}) collective-permute-start(f32[512,256]{1,0:T(8,128)S(1)} %copy-done), channel_id=1, source_target_pairs={{0,1},{1,0},{2,3},{3,2},{4,5},{5,4},{6,7},{7,6},{8,9},{9,8},{10,11... | collective-permute-start | bytes 1572872 | tf_op jit(solution)/shard_map/ppermute | solution.py:40
  115.7 10.4 %collective-permute-start.22 = (f32[512,256]{1,0:T(8,128)S(1)}, f32[512,256]{1,0:T(8,128)S(1)}, u32[]{:S(2)}, u32[]{:S(2)}) collective-permute-start(f32[512,256]{1,0:T(8,128)S(1)} %collective-permute-done.21.rest_5_.refs_6_), channel_id=1, source_target_pairs={{0,2},{1,3},{2,4},{3,5},{4,6},{5,7},{6,0},{7,1},{8,10},{9,11},{10,... | collective-permute-start | bytes 1572872 | tf_op jit(solution)/shard_map/ppermute | solution.py:37
  115.7 10.4 %collective-permute-start.23 = (f32[512,256]{1,0:T(8,128)S(1)}, f32[512,256]{1,0:T(8,128)S(1)}, u32[]{:S(2)}, u32[]{:S(2)}) collective-permute-start(f32[512,256]{1,0:T(8,128)S(1)} %collective-permute-done.21.rest_5_.refs_6_), channel_id=1, source_target_pairs={{0,6},{1,7},{2,0},{3,1},{4,2},{5,3},{6,4},{7,5},{8,14},{9,15},{10,... | collective-permute-start | bytes 1572872 | tf_op jit(solution)/shard_map/ppermute | solution.py:37
  120.6 10.9 %collective-permute-start.24 = (f32[512,256]{1,0:T(8,128)S(1)}, f32[512,256]{1,0:T(8,128)}, u32[]{:S(2)}, u32[]{:S(2)}) collective-permute-start(f32[512,256]{1,0:T(8,128)S(1)} %constant_dynamic-update-slice_fusion.2.rest_4_.refs_5_), channel_id=1, source_target_pairs={{0,1},{1,0},{2,3},{3,2},{4,5},{5,4},{6,7},{7,6},{8,9},{9,8},{10,11... | collective-permute-start | bytes 1572872 | tf_op jit(solution)/shard_map/ppermute | solution.py:40
  131.5 11.4 %collective-permute-start.28 = (f32[384,256]{1,0:T(8,128)}, f32[384,256]{1,0:T(8,128)S(1)}, u32[]{:S(2)}, u32[]{:S(2)}) collective-permute-start(f32[384,256]{1,0:T(8,128)} %get-tuple-element.30.rest_0_), channel_id=1, source_target_pairs={{0,2},{1,3},{2,4},{3,5},{4,6},{5,7},{6,0},{7,1},{8,10},{9,11},{10,... | collective-permute-start | bytes 1179656 | tf_op jit(solution)/shard_map/ppermute | solution.py:37
  131.7 11.3 %collective-permute-start.30 = (f32[384,256]{1,0:T(8,128)}, f32[384,256]{1,0:T(8,128)S(1)}, u32[]{:S(2)}, u32[]{:S(2)}) collective-permute-start(f32[384,256]{1,0:T(8,128)} %get-tuple-element.30.rest_0_), channel_id=1, source_target_pairs={{0,6},{1,7},{2,0},{3,1},{4,2},{5,3},{6,4},{7,5},{8,14},{9,15},{10,... | collective-permute-start | bytes 1179656 | tf_op jit(solution)/shard_map/ppermute | solution.py:37
  136.2 21.3 %collective-permute-start.25 = (f32[384,256]{1,0:T(8,128)}, f32[384,256]{1,0:T(8,128)S(1)}, u32[]{:S(2)}, u32[]{:S(2)}) collective-permute-start(f32[384,256]{1,0:T(8,128)} %get-tuple-element.30.rest_0_), channel_id=1, source_target_pairs={{0,1},{1,0},{2,3},{3,2},{4,5},{5,4},{6,7},{7,6},{8,9},{9,8},{10,11... | collective-permute-start | bytes 1179656 | tf_op jit(solution)/shard_map/ppermute | solution.py:40
  142.9 17.9 %collective-permute-start.29 = (f32[192,256]{1,0:T(8,128)S(1)}, f32[192,256]{1,0:T(8,128)S(1)}, u32[]{:S(2)}, u32[]{:S(2)}) collective-permute-start(f32[192,256]{1,0:T(8,128)S(1)} %slice.32), channel_id=1, source_target_pairs={{0,2},{1,3},{2,4},{3,5},{4,6},{5,7},{6,0},{7,1},{8,10},{9,11},{10,... | collective-permute-start | bytes 589832 | tf_op jit(solution)/shard_map/ppermute | solution.py:37
  143.0 17.8 %collective-permute-start.31 = (f32[192,256]{1,0:T(8,128)S(1)}, f32[192,256]{1,0:T(8,128)S(1)}, u32[]{:S(2)}, u32[]{:S(2)}) collective-permute-start(f32[192,256]{1,0:T(8,128)S(1)} %slice.33), channel_id=1, source_target_pairs={{0,6},{1,7},{2,0},{3,1},{4,2},{5,3},{6,4},{7,5},{8,14},{9,15},{10,... | collective-permute-start | bytes 589832 | tf_op jit(solution)/shard_map/ppermute | solution.py:37
  157.5 11.2 %collective-permute-start.26 = (f32[384,256]{1,0:T(8,128)S(1)}, f32[384,256]{1,0:T(8,128)S(1)}, u32[]{:S(2)}, u32[]{:S(2)}) collective-permute-start(f32[384,256]{1,0:T(8,128)S(1)} %collective-permute-done.25.rest_4_), channel_id=1, source_target_pairs={{0,2},{1,3},{2,4},{3,5},{4,6},{5,7},{6,0},{7,1},{8,10},{9,11},{10,... | collective-permute-start | bytes 1179656 | tf_op jit(solution)/shard_map/ppermute | solution.py:37
  157.5 11.1 %collective-permute-start.27 = (f32[384,256]{1,0:T(8,128)S(1)}, f32[384,256]{1,0:T(8,128)S(1)}, u32[]{:S(2)}, u32[]{:S(2)}) collective-permute-start(f32[384,256]{1,0:T(8,128)S(1)} %collective-permute-done.25.rest_4_), channel_id=1, source_target_pairs={{0,6},{1,7},{2,0},{3,1},{4,2},{5,3},{6,4},{7,5},{8,14},{9,15},{10,... | collective-permute-start | bytes 1179656 | tf_op jit(solution)/shard_map/ppermute | solution.py:37
  (36 other events, 362.3 us)
Sparse Core Ops, SparseCore 0:
  9.7 34.5 all-gather.4
  46.0 34.2 all-gather.8
  98.9 26.7 all-gather.6
  176.1 37.8 reduce-scatter.1
